TPU v7x, 256 devices: a whole 4x4x8 slice. The times are simulated.
256 devices in a mesh: worker: 4 (over z_hi), fsdp: 64 (over y, x, z_lo, core).
Axes of the slice: x: 4, y: 4, z: 8 (z_hi: 4, z_lo: 2; z = z_hi * 2 + z_lo), core: 2. Of those that a mesh axis runs over, the one named last changes fastest.
Arguments:
- inner_input: bfloat16 [4, 32768, 4608], P('worker', 'fsdp'), may hold values from -16 to 16
- inner_weight: bfloat16 [4, 4608, 1024], P('worker', 'fsdp'), may hold values from -6 to 6
- grad_out: bfloat16 [4, 32768, 1024], P('worker', 'fsdp'), may hold values from -6 to 6
- local_fragment: bfloat16 [4, 4608, 18432], P('worker', 'fsdp'), may hold values from -6 to 6
- anchor: bfloat16 [4608, 18432], P('fsdp'), may hold values from -6 to 6
- momentum: float32 [4608, 18432], P('fsdp', 'worker'), may hold values from -6 to 6
Outputs:
- weight_grad: float32 [4, 4608, 1024], P('worker', 'fsdp')
- new_anchor: bfloat16 [4608, 18432], P('fsdp', 'worker')
- new_momentum: float32 [4608, 18432], P('fsdp', 'worker')
All inputs are finite; a program needn't handle non-finite values.
Results may differ from a plain program's by a relative error of at most 0.0035.
Values may be sent and summed in bfloat16 or wider, within the bound.
A program may use at most 128 MiB of HBM per device.

v0:
```python
import jax
import jax.numpy as jnp
from jax import lax
from jax.sharding import PartitionSpec as P

QBLOCK = 32


def e2m1_level(u):
    level = 0.5 * (u >= 0.25) + 0.5 * (u >= 0.75) + 0.5 * (u >= 1.25) + 0.5 * (u >= 1.75)
    level = level + 1.0 * (u >= 2.5) + 1.0 * (u >= 3.5) + 2.0 * (u >= 5.0)
    return level.astype(u.dtype)


def code_delta(local, anchor):
    delta = anchor.astype(jnp.float32) - local.astype(jnp.float32)
    rows_n, cols_n = delta.shape
    blocks = delta.reshape(rows_n, cols_n // QBLOCK, QBLOCK)
    top = jnp.max(jnp.abs(blocks), axis=2, keepdims=True)
    step = jnp.exp2(jnp.ceil(jnp.log2(top))) * 0.25
    level = e2m1_level(jnp.abs(blocks) / step)
    return (jnp.sign(blocks) * level * step).reshape(rows_n, cols_n)


def inner_window(inner_input, inner_weight, grad_out):
    inputs = inner_input[0]
    factor = inputs.shape[1] ** (-0.5)
    columns = inputs
    pre = (
        jnp.dot(
            columns,
            lax.all_gather(inner_weight[0], "fsdp", axis=0, tiled=True),
            preferred_element_type=jnp.float32,
        )
        * factor
    )
    sig = jax.nn.sigmoid(pre)
    act_grad = (grad_out[0].astype(jnp.float32) * sig * (1.0 + pre * (1.0 - sig))).astype(
        jnp.bfloat16
    )
    columns = inputs
    product = lax.dot_general(
        columns, act_grad, (((0,), (0,)), ((), ())), preferred_element_type=jnp.float32
    )
    grad_rows = lax.psum_scatter(product * factor, "fsdp", scatter_dimension=0, tiled=True)
    return grad_rows[None]


def outer_step(local_fragment, anchor, momentum):
    coded = code_delta(local_fragment[0], anchor)
    total = lax.psum_scatter(
        coded.astype(jnp.bfloat16), "worker", scatter_dimension=1, tiled=True
    ).astype(jnp.float32)
    outer_grad = total / lax.axis_size("worker")
    new_momentum = 0.9 * momentum + outer_grad
    width = momentum.shape[1]
    anchor_part = lax.dynamic_slice_in_dim(
        anchor, lax.axis_index("worker") * width, width, 1
    ).astype(jnp.float32)
    new_anchor = (anchor_part - 0.7 * (outer_grad + 0.9 * new_momentum)).astype(jnp.bfloat16)
    return (new_anchor, new_momentum)


def shards(inner_input, inner_weight, grad_out, local_fragment, anchor, momentum):
    weight_grad = inner_window(inner_input, inner_weight, grad_out)
    new_anchor, new_momentum = outer_step(local_fragment, anchor, momentum)
    return (weight_grad, new_anchor, new_momentum)


def solution(mesh):
    in_specs = (
        P("worker", "fsdp", None),
        P("worker", "fsdp", None),
        P("worker", "fsdp", None),
        P("worker", "fsdp", None),
        P("fsdp", None),
        P("fsdp", "worker"),
    )
    out_specs = (P("worker", "fsdp", None), P("fsdp", "worker"), P("fsdp", "worker"))
    return jax.shard_map(shards, mesh=mesh, in_specs=in_specs, out_specs=out_specs, check_vma=False)
```

profile of v0, /device:TPU:1, one launch (start us, length us, event | category | flops | bytes accessed | tf_op | source)
XLA Modules:
  0.0 565.2 jit_solution(3535117207734897447)
XLA Ops:
  8.0 0.0 copy-start
  8.0 0.0 all-gather.3.cloned.1.call-start
  8.1 0.7 all-gather.3.cloned.1.call-update
  8.7 0.0 reduce-scatter.5.cloned.1.call-start
  8.8 5.9 %copy.17 = bf16[72,18432]{0,1:T(8,128)(2,1)} copy(bf16[72,18432]{1,0:T(8,128)(2,1)} %param.10) | data formatting | bytes 5308416 | tf_op args[4]
  14.7 0.0 copy-done
  14.7 4.0 copy.19
  18.8 8.6 %fusion.3 = f32[72,18432]{0,1:T(8,128)} fusion(bf16[72,18432]{0,1:T(8,128)(2,1)} %copy.17, bf16[1,72,18432]{1,2,0:T(8,128)(2,1)} %copy.19), kind=kLoop, calls=%fused_computation.7 | loop fusion | flops 5308416 | bytes 10616832 | tf_op jit(solution)/shard_map/abs | solution.py:21
  27.4 6.1 %reduce_max.9 = f32[72,576]{0,1:T(8,128)S(1)} reduce(f32[72,576,32]{0,2,1:T(8,128)} %bitcast.34, f32[]{:T(128)} %constant.13.clone.1), dimensions={2}, to_apply=%region_1.0 | reduce | flops 1285632 | bytes 5474308 | tf_op jit(solution)/shard_map/reduce_max | solution.py:19
  33.5 0.1 exponential_multiply_fusion
  33.6 13.7 %fusion = bf16[72,18432]{0,1:T(8,128)(2,1)} fusion(bf16[72,18432]{0,1:T(8,128)(2,1)} %copy.17, bf16[1,72,18432]{1,2,0:T(8,128)(2,1)} %copy.19, f32[72,576]{0,1:T(8,128)S(1)} %exponential_multiply_fusion), kind=kLoop, calls=%fused_computation.3 | loop fusion | flops 38486016 | bytes 8128512 | tf_op jit(solution)/shard_map/convert_element_type | solution.py:52
  47.3 0.0 copy-start.1
  47.3 0.0 reduce-scatter.5.cloned.1.call-update
  47.3 0.0 reduce-scatter.7.cloned.1.call-start
  47.3 152.5 %all-gather.3.cloned.1.call-done = bf16[1,4608,1024]{2,1,0:T(8,128)(2,1)} async-done(((bf16[1,72,1024]{2,1,0:T(8,128)(2,1)}), bf16[1,4608,1024]{2,1,0:T(8,128)(2,1)}) %all-gather.3.cloned.1.call-update) | async-done | bytes 9437200 | tf_op jit(solution)/shard_map/all_gather | solution.py:32
  199.9 0.0 copy-done.1
  199.9 9.6 %fusion.7 = bf16[512,1024]{1,0:T(8,128)(2,1)S(1)} fusion(bf16[1,4608,1024]{2,1,0:T(8,128)(2,1)} %all-gather.3.cloned.1.call-done, bf16[1,512,4608]{2,1,0:T(8,128)(2,1)} %param.6, bf16[1,512,1024]{2,1,0:T(8,128)(2,1)S(1)} %copy-done.1), kind=kOutput, calls=%fused_computation.15 | convolution fusion | flops 4837605376 | bytes 16252928 | tf_op jit(solution)/shard_map/dot_general | solution.py:30
  209.5 11.5 %multiply_bitcast_fusion = f32[4608,1024]{0,1:T(8,128)} fusion(bf16[512,1024]{1,0:T(8,128)(2,1)S(1)} %fusion.7, bf16[1,512,4608]{2,1,0:T(8,128)(2,1)} %param.6), kind=kOutput, calls=%fused_computation | convolution fusion | flops 4836556800 | bytes 24641536 | tf_op jit(solution)/shard_map/dot_general | solution.py:42
  221.0 18.6 %copy.24 = f32[4608,1024]{1,0:T(8,128)} copy(f32[4608,1024]{0,1:T(8,128)} %multiply_bitcast_fusion) | data formatting | bytes 37748736
  239.7 0.0 reduce-scatter.7.cloned.1.call-update
  239.7 1.9 copy.20
  241.6 0.0 reduce-scatter.5.cloned.1.call-done
  241.6 3.8 multiply_add_fusion
  245.4 1.3 copy.22
  246.7 2.8 copy.23
  249.5 306.2 %reduce-scatter.7.cloned.1.call-done = f32[72,1024]{1,0:T(8,128)} async-done(((f32[4608,1024]{1,0:T(8,128)}), f32[72,1024]{1,0:T(8,128)}) %reduce-scatter.7.cloned.1.call-update) | async-done | bytes 294928
  555.7 1.2 copy.25
  556.9 0.9 copy.21
Async XLA Ops:
  8.0 6.7 %copy-start = (bf16[1,72,18432]{2,1,0:T(8,128)(2,1)S(1)}, bf16[1,72,18432]{2,1,0:T(8,128)(2,1)}, u32[]{:S(2)}) copy-start(bf16[1,72,18432]{2,1,0:T(8,128)(2,1)} %param.9) | copy-start | bytes 7962628
  8.0 191.9 %all-gather.3.cloned.1.call-start = ((), (), s32[]{:S(2)}) async-start(), calls=%async_computation.3 | async-start | bytes 9584640 | tf_op jit(solution)/shard_map/all_gather | solution.py:32
  8.7 232.8 %reduce-scatter.5.cloned.1.call-start = ((), (), s32[]{:S(2)}) async-start(), calls=%async_computation.2 | async-start | bytes 5898240 | tf_op jit(solution)/shard_map/reduce_scatter | solution.py:51
  47.3 152.6 %copy-start.1 = (bf16[1,512,1024]{2,1,0:T(8,128)(2,1)S(1)}, bf16[1,512,1024]{2,1,0:T(8,128)(2,1)}, u32[]{:S(2)}) copy-start(bf16[1,512,1024]{2,1,0:T(8,128)(2,1)} %param.8) | copy-start | bytes 3145732
  47.3 508.4 %reduce-scatter.7.cloned.1.call-start = ((), (), s32[]{:S(2)}) async-start(), calls=%async_computation.4 | async-start | bytes 19169280
Sparse Core Ops, SparseCore 0:
  10.7 189.1 all-gather.2
Sparse Core Ops, SparseCore 1:
  47.4 101.0 reduce-scatter.4
  239.8 315.9 reduce-scatter.6
where the time goes:
time: 571 us; the launch traced here: 565 us
  waiting for transfers between devices  460 us (81%)
  local copies, waits for them, and re-layouts  36.6 us (6%)
  other arithmetic  32.3 us (6%)
  matrix products  21.1 us (4%)
  between operations  15.5 us (3%)
    unnamed x4, waiting for transfers between devices  307 us
    all_gather x1, waiting for transfers between devices, inner_window(): lax.all_gather(inner_weight[0], 'fsdp', axis=0, tiled=True)  153 us
    unnamed x12, local copies, waits for them, and re-layouts  36.6 us
    convert_element_type x1, other arithmetic, outer_step(): coded.astype(jnp.bfloat16)  13.7 us
    dot_general x1, matrix products, inner_window(): lax.dot_general(columns, act_grad, (((0,), (0,)), ((), ())), preferred_el...  11.5 us
  transfers between devices with their start and end apart: 3, of which 2 were waited for; matrix products, arithmetic and copies ran while one was open for 16% of the time, Pallas kernels for 0%

commit v1 on v0

v1 whole, which is shorter than its diff:
```python
import jax
import jax.numpy as jnp
from jax import lax
from jax.experimental import pallas as pl
from jax.experimental.pallas import tpu as pltpu
from jax.sharding import PartitionSpec as P

F32 = jnp.float32
BF16 = jnp.bfloat16
MESH = pl.DeviceIdType.MESH

TOK = 512
D = 4608
HALF = 512
Q = 256
YB = 1152
XB = 288
ROWS = 72
WC = 4608
WH = 2304


def ring(i):
    return lax.rem(i + 1, 4), lax.rem(i + 3, 4), lax.rem(i + 2, 4)


def coded_of(local, anchor):
    delta = anchor.astype(F32) - local.astype(F32)
    mag = jnp.abs(delta)
    lane = lax.broadcasted_iota(jnp.int32, mag.shape, 1)
    top = mag
    for s in (1, 2, 4, 8, 16):
        top = jnp.maximum(top, pltpu.roll(top, s, 1))
    top = jnp.where(lax.rem(lane, 32) == 31, top, 0.0)
    for s in (1, 2, 4, 8, 16):
        top = jnp.maximum(top, pltpu.roll(top, 128 - s, 1))
    q = top * (2.0**23 + 1.0)
    low = jnp.abs(q - q * (1.0 - 2.0**-24))
    step = jnp.where(low < top, low * 0.5, low * 0.25)
    level = jnp.where(mag >= 0.25 * step, 0.5, 0.0)
    level = jnp.where(mag >= 0.75 * step, 1.0, level)
    level = jnp.where(mag >= 1.25 * step, 1.5, level)
    level = jnp.where(mag >= 1.75 * step, 2.0, level)
    level = jnp.where(mag >= 2.5 * step, 3.0, level)
    level = jnp.where(mag >= 3.5 * step, 4.0, level)
    level = jnp.where(mag >= 5.0 * step, 6.0, level)
    coded = level * step
    return jnp.where(delta < 0, -coded, coded).astype(BF16)


def kernel(
    x_in, w_in, g_in, loc_in, anc_in, mom_in,
    wg_out, na_out, nm_out,
    xs, gs, wraw, wa, wb, pre, act, pa, pb,
    ra_o, ra_l, ra_r, rb_o, rb_l, rb_r,
    sa, sb, sa16, sb16,
    ta_o, ta_l, ta_r, tb_o, tb_l, tb_r,
    tt, fs_send, fs_recv, fz_send, fz_recv, wg_v,
    loc, anc, mom, cod, wo, wl, wr, na_v, nm_v,
    lsem, ssem, rsem,
):
    me = lax.axis_index("fsdp")
    wk = lax.axis_index("worker")
    c = lax.rem(me, 2)
    z = lax.rem(me // 2, 2)
    x = lax.rem(me // 4, 4)
    y = me // 16
    xr, xl, xo = ring(x)
    yr, yl, yo = ring(y)
    wr_i, wl_i, wo_i = ring(wk)

    def dev(yy, xx, zz, cc):
        return (wk, ((yy * 4 + xx) * 2 + zz) * 2 + cc)

    sib = dev(y, x, z, 1 - c)
    zsame = dev(y, x, 1 - z, c)
    zother = dev(y, x, 1 - z, 1 - c)
    xright, xleft = dev(y, xr, z, c), dev(y, xl, z, c)
    yright, yleft = dev(yr, x, z, c), dev(yl, x, z, c)
    wright, wleft = (wr_i, me), (wl_i, me)

    pending = []
    count = [0]

    def send(src, dst, to):
        k = count[0]
        count[0] += 1
        copy = pltpu.make_async_remote_copy(
            src_ref=src, dst_ref=dst, send_sem=ssem.at[k], recv_sem=rsem.at[k],
            device_id=to, device_id_type=MESH,
        )
        copy.start()
        pending.append(copy)
        return copy

    lcount = [0]

    def local(src, dst):
        k = lcount[0]
        lcount[0] += 1
        copy = pltpu.make_async_copy(src, dst, lsem.at[k])
        copy.start()
        return copy

    def cols(j):
        return pl.ds(pl.multiple_of(j * HALF, HALF), HALF)

    def wcols(j):
        return pl.ds(pl.multiple_of(j * WC, 128), WC)

    def xrows(j):
        return pl.ds(pl.multiple_of(j * XB, 16), XB)

    def xrows_half(j, h):
        return pl.ds(pl.multiple_of(j * XB + h * (XB // 2), 16), XB // 2)

    own_w = local(w_in.at[:, cols(c)], wraw.at[z, c])
    frag = {}
    for name, j in (("o", wo_i), ("r", wr_i), ("l", wl_i), ("s", wk)):
        frag[name] = (
            local(loc_in.at[:, wcols(j)], loc.at[j]),
            local(anc_in.at[:, wcols(j)], anc.at[j]),
        )
    own_x = local(x_in, xs.at[0])
    own_g = local(g_in.at[:, cols(c)], gs.at[0])
    own_m = local(mom_in, mom)

    barrier = pltpu.get_barrier_semaphore()
    partners = (sib, zsame, zother, xright, xleft, yright, yleft, wright, wleft)
    for p in partners:
        pl.semaphore_signal(barrier, inc=1, device_id=p, device_id_type=MESH)
    pl.semaphore_wait(barrier, len(partners))

    g1 = send(w_in.at[:, cols(c)], wraw.at[z, c], zsame)
    g2 = send(w_in.at[:, cols(1 - c)], wraw.at[z, c], zother)
    g0 = send(w_in.at[:, cols(1 - c)], wraw.at[z, c], sib)
    sx = send(x_in, xs.at[1], sib)
    sg = send(g_in.at[:, cols(1 - c)], gs.at[1], sib)

    def code_block(name, j):
        for copy in frag[name]:
            copy.wait()
        for h in range(2):
            def body(i, carry, h=h):
                at = pl.multiple_of(h * WH + i * 128, 128)
                to = pl.multiple_of(i * 128, 128)
                cod[j, h, :, pl.ds(to, 128)] = coded_of(
                    loc[j, :, pl.ds(at, 128)], anc[j, :, pl.ds(at, 128)]
                )
                return carry
            lax.fori_loop(0, WH // 128, body, 0)

    code_block("o", wo_i)
    w0 = send(cod.at[wo_i, 0], wo.at[0], wright)
    w1 = send(cod.at[wo_i, 1], wo.at[1], wleft)

    own_w.wait()
    for copy in (g1, g2, g0):
        copy.wait_recv()
    for zz in range(2):
        rows = jnp.concatenate(
            [wraw[zz, 0].astype(F32), wraw[zz, 1].astype(F32)], axis=0
        ).astype(BF16)
        wa[y, xrows_half(x, zz), :] = rows[:, :Q]
        wb[y, xrows_half(x, zz), :] = rows[:, Q:]

    a1 = send(wa.at[y, xrows(x)], wa.at[y, xrows(x)], xright)
    a2 = send(wa.at[y, xrows(x)], wa.at[y, xrows(x)], xleft)
    b1 = send(wb.at[y, xrows(x)], wb.at[y, xrows(x)], yright)
    b2 = send(wb.at[y, xrows(x)], wb.at[y, xrows(x)], yleft)

    code_block("r", wr_i)
    w2 = send(cod.at[wr_i, 1], wl.at[1], wright)

    a1.wait_recv()
    a3 = send(wa.at[y, xrows_half(xl, 0)], wa.at[y, xrows_half(xl, 0)], xright)
    b1.wait_recv()
    b3 = send(wb.at[yl, xrows_half(x, 0)], wb.at[yl, xrows_half(x, 0)], yright)
    a2.wait_recv()
    a4 = send(wa.at[y, xrows_half(xr, 1)], wa.at[y, xrows_half(xr, 1)], xleft)
    b2.wait_recv()
    b4 = send(wb.at[yr, xrows_half(x, 1)], wb.at[yr, xrows_half(x, 1)], yleft)

    code_block("l", wl_i)
    w3 = send(cod.at[wl_i, 0], wr.at[0], wleft)

    a3.wait_recv()
    a4.wait_recv()
    a5 = send(wa.at[y], wa.at[y], yright)
    a6 = send(wa.at[y], wa.at[y], yleft)
    b3.wait_recv()
    b4.wait_recv()
    b5 = send(wb.at[:, xrows(x)], wb.at[:, xrows(x)], xright)
    b6 = send(wb.at[:, xrows(x)], wb.at[:, xrows(x)], xleft)

    code_block("s", wk)

    def project(w, yy, col, first):
        def body(i, carry):
            t = i // 2
            r = pl.ds(pl.multiple_of(lax.rem(i, 2) * 256, 256), 256)
            lhs = xs[t, r, pl.ds(pl.multiple_of(yy * YB, 128), YB)]
            part = jnp.dot(lhs, w[yy], preferred_element_type=F32)
            if first:
                pre[t, r, col:col + Q] = part
            else:
                pre[t, r, col:col + Q] += part
            return carry
        lax.fori_loop(0, 4, body, 0)

    own_x.wait()
    sx.wait_recv()
    project(wa, y, 0, True)

    a5.wait_recv()
    a7 = send(wa.at[yl, 0:YB // 2], wa.at[yl, 0:YB // 2], yright)
    a6.wait_recv()
    a8 = send(wa.at[yr, YB // 2:YB], wa.at[yr, YB // 2:YB], yleft)
    b5.wait_recv()
    b7 = send(wb.at[0:2, xrows(xl)], wb.at[0:2, xrows(xl)], xright)
    b6.wait_recv()
    b8 = send(wb.at[2:4, xrows(xr)], wb.at[2:4, xrows(xr)], xleft)

    w0.wait_recv()
    w1.wait_recv()
    for j, h in ((wr_i, 0), (wl_i, 1)):
        def body(i, carry, j=j, h=h):
            at = pl.ds(pl.multiple_of(i * 256, 256), 256)
            cod[j, h, :, at] = (cod[j, h, :, at].astype(F32) + wo[h, :, at].astype(F32)).astype(BF16)
            return carry
        lax.fori_loop(0, WH // 256, body, 0)
    w4 = send(cod.at[wr_i, 0], wl.at[0], wright)
    w5 = send(cod.at[wl_i, 1], wr.at[1], wleft)

    project(wa, yl, 0, False)
    project(wa, yr, 0, False)
    a7.wait_recv()
    a8.wait_recv()
    project(wa, yo, 0, False)
    b7.wait_recv()
    b8.wait_recv()
    project(wb, 0, Q, True)
    for yy in (1, 2, 3):
        project(wb, yy, Q, False)

    own_g.wait()
    sg.wait_recv()
    factor = D ** (-0.5)

    def activate(i, carry):
        t = i // 8
        r = pl.ds(pl.multiple_of(lax.rem(i, 8) * 64, 64), 64)
        value = pre[t, r, :] * factor
        sig = jax.nn.sigmoid(value)
        act[t, r, :] = (gs[t, r, :].astype(F32) * sig * (1.0 + value * (1.0 - sig))).astype(BF16)
        return carry

    lax.fori_loop(0, 16, activate, 0)

    def backward(yy, out, col):
        def body(i, carry):
            at = pl.ds(pl.multiple_of(yy * YB + i * 384, 128), 384)
            dims = (((0,), (0,)), ((), ()))
            part = lax.dot_general(xs[0, :, at], act[0, :, col:col + Q], dims, preferred_element_type=F32)
            part += lax.dot_general(xs[1, :, at], act[1, :, col:col + Q], dims, preferred_element_type=F32)
            out[yy, pl.ds(pl.multiple_of(i * 384, 384), 384), :] = part.astype(BF16)
            return carry
        lax.fori_loop(0, 3, body, 0)

    hy = YB // 2
    backward(yo, pa, 0)
    ra0 = send(pa.at[yo, 0:hy], ra_o.at[0], yright)
    ra1 = send(pa.at[yo, hy:YB], ra_o.at[1], yleft)
    backward(yr, pa, 0)
    ra2 = send(pa.at[yr, hy:YB], ra_l.at[hy:YB], yright)
    backward(yl, pa, 0)
    ra3 = send(pa.at[yl, 0:hy], ra_r.at[0:hy], yleft)
    for yy in range(4):
        backward(yy, pb, Q)
    rb0 = send(pb.at[0:2, xrows(xo)], rb_o.at[0], xright)
    rb1 = send(pb.at[2:4, xrows(xo)], rb_o.at[1], xleft)
    rb2 = send(pb.at[2:4, xrows(xr)], rb_l.at[2:4], xright)
    rb3 = send(pb.at[0:2, xrows(xl)], rb_r.at[0:2], xleft)
    backward(y, pa, 0)

    def add_rows(dst, at, other, n):
        def body(i, carry):
            r = pl.ds(pl.multiple_of(i * 96, 16), 96)
            d = pl.ds(pl.multiple_of(at[1] + i * 96, 16), 96)
            dst[at[0], d, :] = (dst[at[0], d, :].astype(F32) + other(r).astype(F32)).astype(BF16)
            return carry
        lax.fori_loop(0, n // 96, body, 0)

    ra0.wait_recv()
    add_rows(pa, (yr, 0), lambda r: ra_o[0, r, :], hy)
    ra4 = send(pa.at[yr, 0:hy], ra_l.at[0:hy], yright)
    ra1.wait_recv()
    add_rows(pa, (yl, hy), lambda r: ra_o[1, r, :], hy)
    ra5 = send(pa.at[yl, hy:YB], ra_r.at[hy:YB], yleft)
    rb0.wait_recv()
    for k in range(2):
        add_rows(pb, (k, xr * XB), lambda r, k=k: rb_o[0, k, r, :], XB)
    rb4 = send(pb.at[0:2, xrows(xr)], rb_l.at[0:2], xright)
    rb1.wait_recv()
    for k in range(2):
        add_rows(pb, (2 + k, xl * XB), lambda r, k=k: rb_o[1, k, r, :], XB)
    rb5 = send(pb.at[2:4, xrows(xl)], rb_r.at[2:4], xleft)

    for copy in (w2, w3, w4, w5):
        copy.wait_recv()
    own_m.wait()
    for h in range(2):
        def outer(i, carry, h=h):
            at = pl.ds(pl.multiple_of(i * 128, 128), 128)
            to = pl.ds(pl.multiple_of(h * WH + i * 128, 128), 128)
            total = cod[wk, h, :, at].astype(F32) + wl[h, :, at].astype(F32) + wr[h, :, at].astype(F32)
            grad = total * 0.25
            fresh = 0.9 * mom[:, to] + grad
            nm_v[:, to] = fresh
            na_v[:, to] = (anc[wk, :, to].astype(F32) - 0.7 * (grad + 0.9 * fresh)).astype(BF16)
            return carry
        lax.fori_loop(0, WH // 128, outer, 0)
    out1 = local(na_v, na_out)
    out2 = local(nm_v, nm_out)

    for copy in (ra2, ra3, ra4, ra5):
        copy.wait_recv()

    def sum_a(i, carry):
        r = pl.ds(pl.multiple_of(i * 96, 96), 96)
        total = pa[y, r, :].astype(F32) + ra_l[r, :].astype(F32) + ra_r[r, :].astype(F32)
        sa[r, :] = total
        sa16[r, :] = total.astype(BF16)
        return carry

    lax.fori_loop(0, YB // 96, sum_a, 0)
    hx = XB // 2
    ta0 = send(sa16.at[xrows_half(xo, 0)], ta_o.at[0], xright)
    ta1 = send(sa16.at[xrows_half(xo, 1)], ta_o.at[1], xleft)
    ta2 = send(sa16.at[xrows_half(xr, 1)], ta_l.at[hx:XB], xright)
    ta3 = send(sa16.at[xrows_half(xl, 0)], ta_r.at[0:hx], xleft)

    for copy in (rb2, rb3, rb4, rb5):
        copy.wait_recv()

    def sum_b(i, carry):
        k = i // 3
        r = pl.ds(pl.multiple_of(lax.rem(i, 3) * 96, 96), 96)
        at = pl.ds(pl.multiple_of(x * XB + lax.rem(i, 3) * 96, 16), 96)
        total = pb[k, at, :].astype(F32) + rb_l[k, r, :].astype(F32) + rb_r[k, r, :].astype(F32)
        sb[k, r, :] = total
        sb16[k, r, :] = total.astype(BF16)
        return carry

    lax.fori_loop(0, 12, sum_b, 0)
    tb0 = send(sb16.at[yo, 0:hx], tb_o.at[0], yright)
    tb1 = send(sb16.at[yo, hx:XB], tb_o.at[1], yleft)
    tb2 = send(sb16.at[yr, hx:XB], tb_l.at[hx:XB], yright)
    tb3 = send(sb16.at[yl, 0:hx], tb_r.at[0:hx], yleft)

    ta0.wait_recv()
    sa16[xrows_half(xr, 0), :] = (sa[xrows_half(xr, 0), :] + ta_o[0].astype(F32)).astype(BF16)
    ta4 = send(sa16.at[xrows_half(xr, 0)], ta_l.at[0:hx], xright)
    ta1.wait_recv()
    sa16[xrows_half(xl, 1), :] = (sa[xrows_half(xl, 1), :] + ta_o[1].astype(F32)).astype(BF16)
    ta5 = send(sa16.at[xrows_half(xl, 1)], ta_r.at[hx:XB], xleft)
    tb0.wait_recv()
    sb16[yr, 0:hx, :] = (sb[yr, 0:hx, :] + tb_o[0].astype(F32)).astype(BF16)
    tb4 = send(sb16.at[yr, 0:hx], tb_l.at[0:hx], yright)
    tb1.wait_recv()
    sb16[yl, hx:XB, :] = (sb[yl, hx:XB, :] + tb_o[1].astype(F32)).astype(BF16)
    tb5 = send(sb16.at[yl, hx:XB], tb_r.at[hx:XB], yleft)

    for copy in (ta2, ta3, ta4, ta5):
        copy.wait_recv()
    tt[:, 0:Q] = sa[xrows(x), :] + ta_l[...].astype(F32) + ta_r[...].astype(F32)
    for copy in (tb2, tb3, tb4, tb5):
        copy.wait_recv()
    tt[:, Q:HALF] = sb[y] + tb_l[...].astype(F32) + tb_r[...].astype(F32)

    def part(zz, cc):
        return pl.ds(pl.multiple_of((zz * 2 + cc) * ROWS, 8), ROWS)

    for k in range(2):
        fz_send[k] = tt[part(1 - z, k), :].astype(BF16)
    f1 = send(fz_send.at[c], fz_recv.at[c], zsame)
    f2 = send(fz_send.at[1 - c], fz_recv.at[c], zother)
    fs_send[...] = tt[part(z, 1 - c), :]
    f0 = send(fs_send, fs_recv, sib)
    for copy in (f1, f2, f0):
        copy.wait_recv()
    wg_v[:, cols(c)] = (tt[part(z, c), :] + fz_recv[c].astype(F32)) * factor
    wg_v[:, cols(1 - c)] = (fs_recv[...] + fz_recv[1 - c].astype(F32)) * factor
    out0 = local(wg_v, wg_out)
    for copy in pending:
        copy.wait_send()
    for copy in (out0, out1, out2):
        copy.wait()


def shards(inner_input, inner_weight, grad_out, local_fragment, anchor, momentum):
    any_spec = pl.BlockSpec(memory_space=pl.ANY)
    vm = pltpu.VMEM
    hx = XB // 2
    wg, na, nm = pl.pallas_call(
        kernel,
        out_shape=(
            jax.ShapeDtypeStruct((ROWS, 1024), F32),
            jax.ShapeDtypeStruct((ROWS, WC), BF16),
            jax.ShapeDtypeStruct((ROWS, WC), F32),
        ),
        in_specs=[any_spec] * 6,
        out_specs=(any_spec,) * 3,
        scratch_shapes=[
            vm((2, TOK, D), BF16), vm((2, TOK, HALF), BF16), vm((2, 2, ROWS, HALF), BF16),
            vm((4, YB, Q), BF16), vm((4, YB, Q), BF16),
            vm((2, TOK, HALF), F32), vm((2, TOK, HALF), BF16),
            vm((4, YB, Q), BF16), vm((4, YB, Q), BF16),
            vm((2, YB // 2, Q), BF16), vm((YB, Q), BF16), vm((YB, Q), BF16),
            vm((2, 2, XB, Q), BF16), vm((4, XB, Q), BF16), vm((4, XB, Q), BF16),
            vm((YB, Q), F32), vm((4, XB, Q), F32), vm((YB, Q), BF16), vm((4, XB, Q), BF16),
            vm((2, hx, Q), BF16), vm((XB, Q), BF16), vm((XB, Q), BF16),
            vm((2, hx, Q), BF16), vm((XB, Q), BF16), vm((XB, Q), BF16),
            vm((XB, HALF), F32),
            vm((ROWS, HALF), F32), vm((ROWS, HALF), F32),
            vm((2, ROWS, HALF), BF16), vm((2, ROWS, HALF), BF16),
            vm((ROWS, 1024), F32),
            vm((4, ROWS, WC), BF16), vm((4, ROWS, WC), BF16), vm((ROWS, WC), F32),
            vm((4, 2, ROWS, WH), BF16),
            vm((2, ROWS, WH), BF16), vm((2, ROWS, WH), BF16), vm((2, ROWS, WH), BF16),
            vm((ROWS, WC), BF16), vm((ROWS, WC), F32),
            pltpu.SemaphoreType.DMA((16,)),
            pltpu.SemaphoreType.DMA((56,)),
            pltpu.SemaphoreType.DMA((56,)),
        ],
        compiler_params=pltpu.CompilerParams(
            collective_id=0, has_side_effects=True, vmem_limit_bytes=60 * 1024 * 1024
        ),
        cost_estimate=pl.CostEstimate(
            flops=4 * TOK * D * 1024, bytes_accessed=16 * 1024 * 1024, transcendentals=TOK * 1024
        ),
    )(inner_input[0], inner_weight[0], grad_out[0], local_fragment[0], anchor, momentum)
    return (wg[None], na, nm)


def solution(mesh):
    in_specs = (
        P("worker", "fsdp", None),
        P("worker", "fsdp", None),
        P("worker", "fsdp", None),
        P("worker", "fsdp", None),
        P("fsdp", None),
        P("fsdp", "worker"),
    )
    out_specs = (P("worker", "fsdp", None), P("fsdp", "worker"), P("fsdp", "worker"))
    return jax.shard_map(shards, mesh=mesh, in_specs=in_specs, out_specs=out_specs, check_vma=False)
```

time: 571 us -> 184 us (0.32)
  waiting for transfers between devices: 460 us -> 0 us
  Pallas kernels: 0 us -> 178 us
  other arithmetic: 32.3 us -> 0 us
  local copies, waits for them, and re-layouts: 36.6 us -> 4.83 us
  matrix products: 21.1 us -> 0 us
  between operations: 15.5 us -> 0.65 us
    unnamed x4 -> x0, waiting for transfers between devices: 307 us -> none
    pallas_call x0 -> x1, Pallas kernels: none -> 178 us  [shards(): pl.pallas_call(kernel, out_shape=(jax.ShapeDtypeStruct((ROWS, 1024), F32)...]
    all_gather x1 -> x0, waiting for transfers between devices: 153 us -> none  [inner_window(): lax.all_gather(inner_weight[0], 'fsdp', axis=0, tiled=True)]
    unnamed x12 -> x5, local copies, waits for them, and re-layouts: 36.6 us -> 4.83 us
    dot_general x2 -> x0, matrix products: 21.1 us -> none  [the longest x1 11.5 us: inner_window(): lax.dot_general(columns, act_grad, (((0,), (0,)), ((), ())), preferred_el...]
    convert_element_type x1 -> x0, other arithmetic: 13.7 us -> none  [outer_step(): coded.astype(jnp.bfloat16)]
    abs x1 -> x0, other arithmetic: 8.62 us -> none  [code_delta(): level = e2m1_level(jnp.abs(blocks) / step)]
    reduce_max x1 -> x0, other arithmetic: 6.12 us -> none  [code_delta(): top = jnp.max(jnp.abs(blocks), axis=2, keepdims=True)]
  transfers between devices with their start and end apart: 3 -> 0, of which waited for: 2 -> 0; matrix products, arithmetic and copies ran while one was open for 16% -> 0% of each run, Pallas kernels for 0% -> 0%
where the time goes in v1:
time: 184 us
  Pallas kernels  178 us (97%)
  local copies, waits for them, and re-layouts  4.83 us (3%)
    pallas_call x1, Pallas kernels, shards(): pl.pallas_call(kernel, out_shape=(jax.ShapeDtypeStruct((ROWS, 1024), F32)...  178 us
    unnamed x5, local copies, waits for them, and re-layouts  4.83 us

profile of v1, /device:TPU:1, one launch (start us, length us, event | category | flops | bytes accessed | tf_op | source)
XLA Modules:
  0.0 183.9 jit_solution(9128310147197283768)
XLA Ops:
  0.6 178.4 %shard_map.85 = (f32[72,1024]{1,0:T(8,128)}, bf16[72,4608]{1,0:T(8,128)(2,1)}, f32[72,4608]{1,0:T(8,128)}) custom-call(bf16[512,4608]{1,0:T(8,128)(2,1)} %bitcast.6, bf16[72,1024]{1,0:T(8,128)(2,1)} %bitcast.9, bf16[512,1024]{1,0:T(8,128)(2,1)} %bitcast.8, bf16[72,18432]{1,0:T(8,128)(2,1)} %bitcast.7, bf16[72,18432]{1,0:T(8,128)(2,1)} %anc_in.1, ...), custom_call_target="tpu_custom_call" | custom-call | flops 9663676416 | bytes 16777216 | tf_op jit(solution)/shard_map/pallas_call | solution.py:405
  179.0 0.0 copy-start
  179.0 1.8 copy.12
  180.8 2.0 %copy.13 = bf16[72,4608]{1,0:T(8,128)(2,1)} copy(bf16[72,4608]{1,0:T(8,128)(2,1)} %get-tuple-element.13) | data formatting | bytes 1327104
  182.8 0.0 copy-done
  182.8 1.1 copy.14
Async XLA Ops:
  179.0 3.8 %copy-start = (f32[72,4608]{1,0:T(8,128)S(1)}, f32[72,4608]{1,0:T(8,128)}, u32[]{:S(2)}) copy-start(f32[72,4608]{1,0:T(8,128)} %get-tuple-element.14) | copy-start | bytes 3981316

commit v2 on v1

--- a/solution.py
+++ b/solution.py
@@ -18,25 +18,21 @@
 ROWS = 72
 WC = 4608
 WH = 2304
+SETS = 3
 
 
 def ring(i):
     return lax.rem(i + 1, 4), lax.rem(i + 3, 4), lax.rem(i + 2, 4)
 
 
-def coded_of(local, anchor):
-    delta = anchor.astype(F32) - local.astype(F32)
-    mag = jnp.abs(delta)
-    lane = lax.broadcasted_iota(jnp.int32, mag.shape, 1)
-    top = mag
-    for s in (1, 2, 4, 8, 16):
-        top = jnp.maximum(top, pltpu.roll(top, s, 1))
-    top = jnp.where(lax.rem(lane, 32) == 31, top, 0.0)
-    for s in (1, 2, 4, 8, 16):
-        top = jnp.maximum(top, pltpu.roll(top, 128 - s, 1))
+def step_of(top):
     q = top * (2.0**23 + 1.0)
     low = jnp.abs(q - q * (1.0 - 2.0**-24))
-    step = jnp.where(low < top, low * 0.5, low * 0.25)
+    return jnp.where(low < top, low * 0.5, low * 0.25)
+
+
+def coded_of(delta, step):
+    mag = jnp.abs(delta)
     level = jnp.where(mag >= 0.25 * step, 0.5, 0.0)
     level = jnp.where(mag >= 0.75 * step, 1.0, level)
     level = jnp.where(mag >= 1.25 * step, 1.5, level)
@@ -46,6 +42,36 @@
     level = jnp.where(mag >= 5.0 * step, 6.0, level)
     coded = level * step
     return jnp.where(delta < 0, -coded, coded).astype(BF16)
+
+
+def merge(a, b, bit, s):
+    keep = jnp.where(bit, b, a)
+    move = jnp.where(bit, pltpu.roll(b, s, 1), pltpu.roll(a, 128 - s, 1))
+    return jnp.maximum(keep, move)
+
+
+def code_chunk(delta_at, store):
+    lane = lax.broadcasted_iota(jnp.int32, (ROWS, 128), 1)
+    bit0, bit1, last = (lane & 1) == 1, (lane & 2) == 2, (lane & 28) == 28
+    src = lax.broadcasted_iota(jnp.int32, (128, 512), 0)
+    dst = lax.broadcasted_iota(jnp.int32, (128, 512), 1)
+    spread = jnp.where(src == ((dst & 96) | 28 | (dst // 128)), 1.0, 0.0).astype(BF16)
+    deltas, steps = [], []
+    for k in range(SETS):
+        four = [delta_at(4 * k + g) for g in range(4)]
+        m = [jnp.abs(d) for d in four]
+        top = merge(merge(m[0], m[1], bit0, 1), merge(m[2], m[3], bit0, 1), bit1, 2)
+        for s in (4, 8, 16):
+            top = jnp.maximum(top, pltpu.roll(top, s, 1))
+        steps.append(jnp.where(last, step_of(top), 0.0))
+        deltas.append(four)
+    spread_steps = jnp.dot(
+        jnp.concatenate(steps, axis=0).astype(BF16), spread, preferred_element_type=F32
+    )
+    for k in range(SETS):
+        for g in range(4):
+            step = spread_steps[ROWS * k:ROWS * (k + 1), 128 * g:128 * (g + 1)]
+            store(4 * k + g, coded_of(deltas[k][g], step))
 
 
 def kernel(
@@ -108,6 +134,9 @@
     def wcols(j):
         return pl.ds(pl.multiple_of(j * WC, 128), WC)
 
+    def half(ref, h):
+        return ref.at[:, h * WH:(h + 1) * WH]
+
     def xrows(j):
         return pl.ds(pl.multiple_of(j * XB, 16), XB)
 
@@ -140,19 +169,23 @@
     def code_block(name, j):
         for copy in frag[name]:
             copy.wait()
-        for h in range(2):
-            def body(i, carry, h=h):
-                at = pl.multiple_of(h * WH + i * 128, 128)
-                to = pl.multiple_of(i * 128, 128)
-                cod[j, h, :, pl.ds(to, 128)] = coded_of(
-                    loc[j, :, pl.ds(at, 128)], anc[j, :, pl.ds(at, 128)]
-                )
-                return carry
-            lax.fori_loop(0, WH // 128, body, 0)
+        def body(i, carry):
+            def at(g):
+                return pl.ds(pl.multiple_of((i * (4 * SETS) + g) * 128, 128), 128)
+
+            def delta_at(g):
+                return anc[j, :, at(g)].astype(F32) - loc[j, :, at(g)].astype(F32)
+
+            def store(g, value):
+                cod[j, :, at(g)] = value
+
+            code_chunk(delta_at, store)
+            return carry
+        lax.fori_loop(0, WC // (512 * SETS), body, 0)
 
     code_block("o", wo_i)
-    w0 = send(cod.at[wo_i, 0], wo.at[0], wright)
-    w1 = send(cod.at[wo_i, 1], wo.at[1], wleft)
+    w0 = send(half(cod.at[wo_i], 0), wo.at[0], wright)
+    w1 = send(half(cod.at[wo_i], 1), wo.at[1], wleft)
 
     own_w.wait()
     for copy in (g1, g2, g0):
@@ -170,7 +203,7 @@
     b2 = send(wb.at[y, xrows(x)], wb.at[y, xrows(x)], yleft)
 
     code_block("r", wr_i)
-    w2 = send(cod.at[wr_i, 1], wl.at[1], wright)
+    w2 = send(half(cod.at[wr_i], 1), half(wl, 1), wright)
 
     a1.wait_recv()
     a3 = send(wa.at[y, xrows_half(xl, 0)], wa.at[y, xrows_half(xl, 0)], xright)
@@ -182,7 +215,7 @@
     b4 = send(wb.at[yr, xrows_half(x, 1)], wb.at[yr, xrows_half(x, 1)], yleft)
 
     code_block("l", wl_i)
-    w3 = send(cod.at[wl_i, 0], wr.at[0], wleft)
+    w3 = send(half(cod.at[wl_i], 0), half(wr, 0), wleft)
 
     a3.wait_recv()
     a4.wait_recv()
@@ -195,22 +228,30 @@
 
     code_block("s", wk)
 
-    def project(w, yy, col, first):
+    def project(yy, first):
+        def body(t, carry):
+            lhs = xs[t, :, pl.ds(pl.multiple_of(yy * YB, 128), YB)]
+            part = jnp.dot(lhs, wa[yy], preferred_element_type=F32)
+            if first:
+                pre[t, :, 0:Q] = part
+            else:
+                pre[t, :, 0:Q] += part
+            return carry
+        lax.fori_loop(0, 2, body, 0)
+
+    def project_rest():
         def body(i, carry):
             t = i // 2
             r = pl.ds(pl.multiple_of(lax.rem(i, 2) * 256, 256), 256)
-            lhs = xs[t, r, pl.ds(pl.multiple_of(yy * YB, 128), YB)]
-            part = jnp.dot(lhs, w[yy], preferred_element_type=F32)
-            if first:
-                pre[t, r, col:col + Q] = part
-            else:
-                pre[t, r, col:col + Q] += part
+            pre[t, r, Q:HALF] = jnp.dot(
+                xs[t, r, :], wb[...].reshape(D, Q), preferred_element_type=F32
+            )
             return carry
         lax.fori_loop(0, 4, body, 0)
 
     own_x.wait()
     sx.wait_recv()
-    project(wa, y, 0, True)
+    project(y, True)
 
     a5.wait_recv()
     a7 = send(wa.at[yl, 0:YB // 2], wa.at[yl, 0:YB // 2], yright)
@@ -226,22 +267,21 @@
     for j, h in ((wr_i, 0), (wl_i, 1)):
         def body(i, carry, j=j, h=h):
             at = pl.ds(pl.multiple_of(i * 256, 256), 256)
-            cod[j, h, :, at] = (cod[j, h, :, at].astype(F32) + wo[h, :, at].astype(F32)).astype(BF16)
+            to = pl.ds(pl.multiple_of(h * WH + i * 256, 256), 256)
+            cod[j, :, to] = (cod[j, :, to].astype(F32) + wo[h, :, at].astype(F32)).astype(BF16)
             return carry
         lax.fori_loop(0, WH // 256, body, 0)
-    w4 = send(cod.at[wr_i, 0], wl.at[0], wright)
-    w5 = send(cod.at[wl_i, 1], wr.at[1], wleft)
-
-    project(wa, yl, 0, False)
-    project(wa, yr, 0, False)
+    w4 = send(half(cod.at[wr_i], 0), half(wl, 0), wright)
+    w5 = send(half(cod.at[wl_i], 1), half(wr, 1), wleft)
+
+    project(yl, False)
+    project(yr, False)
     a7.wait_recv()
     a8.wait_recv()
-    project(wa, yo, 0, False)
+    project(yo, False)
     b7.wait_recv()
     b8.wait_recv()
-    project(wb, 0, Q, True)
-    for yy in (1, 2, 3):
-        project(wb, yy, Q, False)
+    project_rest()
 
     own_g.wait()
     sg.wait_recv()
@@ -258,14 +298,11 @@
     lax.fori_loop(0, 16, activate, 0)
 
     def backward(yy, out, col):
-        def body(i, carry):
-            at = pl.ds(pl.multiple_of(yy * YB + i * 384, 128), 384)
-            dims = (((0,), (0,)), ((), ()))
-            part = lax.dot_general(xs[0, :, at], act[0, :, col:col + Q], dims, preferred_element_type=F32)
-            part += lax.dot_general(xs[1, :, at], act[1, :, col:col + Q], dims, preferred_element_type=F32)
-            out[yy, pl.ds(pl.multiple_of(i * 384, 384), 384), :] = part.astype(BF16)
-            return carry
-        lax.fori_loop(0, 3, body, 0)
+        at = pl.ds(pl.multiple_of(yy * YB, 128), YB)
+        dims = (((0,), (0,)), ((), ()))
+        part = lax.dot_general(xs[0, :, at], act[0, :, col:col + Q], dims, preferred_element_type=F32)
+        part += lax.dot_general(xs[1, :, at], act[1, :, col:col + Q], dims, preferred_element_type=F32)
+        out[yy] = part.astype(BF16)
 
     hy = YB // 2
     backward(yo, pa, 0)
@@ -275,8 +312,12 @@
     ra2 = send(pa.at[yr, hy:YB], ra_l.at[hy:YB], yright)
     backward(yl, pa, 0)
     ra3 = send(pa.at[yl, 0:hy], ra_r.at[0:hy], yleft)
-    for yy in range(4):
+
+    def backward_rest(yy, carry):
         backward(yy, pb, Q)
+        return carry
+
+    lax.fori_loop(0, 4, backward_rest, 0)
     rb0 = send(pb.at[0:2, xrows(xo)], rb_o.at[0], xright)
     rb1 = send(pb.at[2:4, xrows(xo)], rb_o.at[1], xleft)
     rb2 = send(pb.at[2:4, xrows(xr)], rb_l.at[2:4], xright)
@@ -309,17 +350,17 @@
     for copy in (w2, w3, w4, w5):
         copy.wait_recv()
     own_m.wait()
-    for h in range(2):
-        def outer(i, carry, h=h):
-            at = pl.ds(pl.multiple_of(i * 128, 128), 128)
-            to = pl.ds(pl.multiple_of(h * WH + i * 128, 128), 128)
-            total = cod[wk, h, :, at].astype(F32) + wl[h, :, at].astype(F32) + wr[h, :, at].astype(F32)
-            grad = total * 0.25
-            fresh = 0.9 * mom[:, to] + grad
-            nm_v[:, to] = fresh
-            na_v[:, to] = (anc[wk, :, to].astype(F32) - 0.7 * (grad + 0.9 * fresh)).astype(BF16)
-            return carry
-        lax.fori_loop(0, WH // 128, outer, 0)
+
+    def outer(i, carry):
+        at = pl.ds(pl.multiple_of(i * 256, 256), 256)
+        total = cod[wk, :, at].astype(F32) + wl[:, at].astype(F32) + wr[:, at].astype(F32)
+        grad = total * 0.25
+        fresh = 0.9 * mom[:, at] + grad
+        nm_v[:, at] = fresh
+        na_v[:, at] = (anc[wk, :, at].astype(F32) - 0.7 * (grad + 0.9 * fresh)).astype(BF16)
+        return carry
+
+    lax.fori_loop(0, WC // 256, outer, 0)
     out1 = local(na_v, na_out)
     out2 = local(nm_v, nm_out)
 
@@ -426,8 +467,8 @@
             vm((2, ROWS, HALF), BF16), vm((2, ROWS, HALF), BF16),
             vm((ROWS, 1024), F32),
             vm((4, ROWS, WC), BF16), vm((4, ROWS, WC), BF16), vm((ROWS, WC), F32),
-            vm((4, 2, ROWS, WH), BF16),
-            vm((2, ROWS, WH), BF16), vm((2, ROWS, WH), BF16), vm((2, ROWS, WH), BF16),
+            vm((4, ROWS, WC), BF16),
+            vm((2, ROWS, WH), BF16), vm((ROWS, WC), BF16), vm((ROWS, WC), BF16),
             vm((ROWS, WC), BF16), vm((ROWS, WC), F32),
             pltpu.SemaphoreType.DMA((16,)),
             pltpu.SemaphoreType.DMA((56,)),

time: 184 us -> 95.9 us (0.52)
  Pallas kernels: 178 us -> 90.3 us
    pallas_call x1, Pallas kernels: 178 us -> 90.3 us  [shards(): pl.pallas_call(kernel, out_shape=(jax.ShapeDtypeStruct((ROWS, 1024), F32)...]
where the time goes in v2:
time: 95.9 us; the launch traced here: 95.8 us
  Pallas kernels  90.3 us (94%)
  local copies, waits for them, and re-layouts  4.83 us (5%)
    pallas_call x1, Pallas kernels, shards(): pl.pallas_call(kernel, out_shape=(jax.ShapeDtypeStruct((ROWS, 1024), F32)...  90.3 us
    unnamed x5, local copies, waits for them, and re-layouts  4.83 us

profile of v2, /device:TPU:1, one launch (start us, length us, event | category | flops | bytes accessed | tf_op | source)
XLA Modules:
  0.0 95.8 jit_solution(17342017924164336112)
XLA Ops:
  0.6 90.3 %shard_map.85 = (f32[72,1024]{1,0:T(8,128)}, bf16[72,4608]{1,0:T(8,128)(2,1)}, f32[72,4608]{1,0:T(8,128)}) custom-call(bf16[512,4608]{1,0:T(8,128)(2,1)} %bitcast.6, bf16[72,1024]{1,0:T(8,128)(2,1)} %bitcast.9, bf16[512,1024]{1,0:T(8,128)(2,1)} %bitcast.8, bf16[72,18432]{1,0:T(8,128)(2,1)} %bitcast.7, bf16[72,18432]{1,0:T(8,128)(2,1)} %anc_in.1, ...), custom_call_target="tpu_custom_call" | custom-call | flops 9663676416 | bytes 16777216 | tf_op jit(solution)/shard_map/pallas_call | solution.py:446
  90.9 0.0 copy-start
  90.9 1.8 %copy.12 = f32[1,72,1024]{2,1,0:T(8,128)} copy(f32[1,72,1024]{2,1,0:T(8,128)} %bitcast.5) | data formatting | bytes 589824
  92.7 2.0 %copy.13 = bf16[72,4608]{1,0:T(8,128)(2,1)} copy(bf16[72,4608]{1,0:T(8,128)(2,1)} %get-tuple-element.13) | data formatting | bytes 1327104
  94.7 0.0 copy-done
  94.7 1.1 %copy.14 = f32[72,4608]{1,0:T(8,128)} copy(f32[72,4608]{1,0:T(8,128)S(1)} %copy-done) | data formatting | bytes 2654208
Async XLA Ops:
  90.9 3.8 %copy-start = (f32[72,4608]{1,0:T(8,128)S(1)}, f32[72,4608]{1,0:T(8,128)}, u32[]{:S(2)}) copy-start(f32[72,4608]{1,0:T(8,128)} %get-tuple-element.14) | copy-start | bytes 3981316

commit v3 on v2

v3 whole, which is shorter than its diff:
```python
import jax
import jax.numpy as jnp
from jax import lax
from jax.experimental import pallas as pl
from jax.experimental.pallas import tpu as pltpu
from jax.sharding import PartitionSpec as P

F32 = jnp.float32
BF16 = jnp.bfloat16
MESH = pl.DeviceIdType.MESH

TOK = 512
D = 4608
HALF = 512
R = 128
YB = 1152
XB = 288
ROWS = 72
WC = 4608
WH = 2304
SETS = 3


def ring(i):
    return lax.rem(i + 1, 4), lax.rem(i + 3, 4), lax.rem(i + 2, 4)


def step_of(top):
    q = top * (2.0**23 + 1.0)
    low = jnp.abs(q - q * (1.0 - 2.0**-24))
    return jnp.where(low < top, low * 0.5, low * 0.25)


def coded_of(delta, step):
    mag = jnp.abs(delta)
    level = jnp.where(mag >= 0.25 * step, 0.5, 0.0)
    level = jnp.where(mag >= 0.75 * step, 1.0, level)
    level = jnp.where(mag >= 1.25 * step, 1.5, level)
    level = jnp.where(mag >= 1.75 * step, 2.0, level)
    level = jnp.where(mag >= 2.5 * step, 3.0, level)
    level = jnp.where(mag >= 3.5 * step, 4.0, level)
    level = jnp.where(mag >= 5.0 * step, 6.0, level)
    coded = level * step
    return jnp.where(delta < 0, -coded, coded).astype(BF16)


def merge(a, b, bit, s):
    keep = jnp.where(bit, b, a)
    move = jnp.where(bit, pltpu.roll(b, s, 1), pltpu.roll(a, 128 - s, 1))
    return jnp.maximum(keep, move)


def code_chunk(delta_at, store):
    lane = lax.broadcasted_iota(jnp.int32, (ROWS, 128), 1)
    bit0, bit1, last = (lane & 1) == 1, (lane & 2) == 2, (lane & 28) == 28
    src = lax.broadcasted_iota(jnp.int32, (128, 512), 0)
    dst = lax.broadcasted_iota(jnp.int32, (128, 512), 1)
    spread = jnp.where(src == ((dst & 96) | 28 | (dst // 128)), 1.0, 0.0).astype(BF16)
    deltas, steps = [], []
    for k in range(SETS):
        four = [delta_at(4 * k + g) for g in range(4)]
        m = [jnp.abs(d) for d in four]
        top = merge(merge(m[0], m[1], bit0, 1), merge(m[2], m[3], bit0, 1), bit1, 2)
        for s in (4, 8, 16):
            top = jnp.maximum(top, pltpu.roll(top, s, 1))
        steps.append(jnp.where(last, step_of(top), 0.0))
        deltas.append(four)
    spread_steps = jnp.dot(
        jnp.concatenate(steps, axis=0).astype(BF16), spread, preferred_element_type=F32
    )
    for k in range(SETS):
        for g in range(4):
            step = spread_steps[ROWS * k:ROWS * (k + 1), 128 * g:128 * (g + 1)]
            store(4 * k + g, coded_of(deltas[k][g], step))


def kernel(
    x_in, w_in, g_in, loc_in, anc_in, mom_in,
    wg_out, na_out, nm_out,
    xs, gs, wraw, wa, wb, act, pa, pb,
    ra_o, ra_l, ra_r, rb_o, rb_l, rb_r,
    sa, sb, sa16, sb16,
    ta_o, ta_l, ta_r, tb_o, tb_l, tb_r,
    tt, fs_send, fs_recv, fz_send, fz_recv, wg_v,
    loc, anc, mom, cod, wo, wl, wr, na_v, nm_v,
    lsem, ssem, rsem,
):
    me = lax.axis_index("fsdp")
    wk = lax.axis_index("worker")
    c = lax.rem(me, 2)
    z = lax.rem(me // 2, 2)
    x = lax.rem(me // 4, 4)
    y = me // 16
    xr, xl, xo = ring(x)
    yr, yl, yo = ring(y)
    wr_i, wl_i, wo_i = ring(wk)
    hy, hx = YB // 2, XB // 2
    factor = D ** (-0.5)

    def dev(yy, xx, zz, cc):
        return (wk, ((yy * 4 + xx) * 2 + zz) * 2 + cc)

    sib = dev(y, x, z, 1 - c)
    zsame = dev(y, x, 1 - z, c)
    zother = dev(y, x, 1 - z, 1 - c)
    xright, xleft = dev(y, xr, z, c), dev(y, xl, z, c)
    yright, yleft = dev(yr, x, z, c), dev(yl, x, z, c)
    wright, wleft = (wr_i, me), (wl_i, me)

    pending = []

    def send(src, dst, to):
        k = len(pending)
        copy = pltpu.make_async_remote_copy(
            src_ref=src, dst_ref=dst, send_sem=ssem.at[k], recv_sem=rsem.at[k],
            device_id=to, device_id_type=MESH,
        )
        copy.start()
        pending.append(copy)
        return copy

    started = []

    def local(src, dst):
        copy = pltpu.make_async_copy(src, dst, lsem.at[len(started)])
        copy.start()
        started.append(copy)
        return copy

    def arrived(*copies):
        for copy in copies:
            copy.wait_recv()

    def cols(j):
        return pl.ds(pl.multiple_of(j * HALF, HALF), HALF)

    def wcols(j):
        return pl.ds(pl.multiple_of(j * WC, 128), WC)

    def half(ref, h):
        return ref.at[:, h * WH:(h + 1) * WH]

    def xrows(j):
        return pl.ds(pl.multiple_of(j * XB, 16), XB)

    def xrows_half(j, h):
        return pl.ds(pl.multiple_of(j * XB + h * hx, 16), hx)

    own_w = local(w_in.at[:, cols(c)], wraw.at[z, c])
    frag = {}
    for name, j in (("o", wo_i), ("r", wr_i), ("l", wl_i), ("s", wk)):
        frag[name] = (
            local(loc_in.at[:, wcols(j)], loc.at[j]),
            local(anc_in.at[:, wcols(j)], anc.at[j]),
        )
    own_x = local(x_in, xs.at[0])
    own_g = local(g_in.at[:, cols(c)], gs.at[0])
    own_m = local(mom_in, mom)

    barrier = pltpu.get_barrier_semaphore()
    partners = (sib, zsame, zother, xright, xleft, yright, yleft, wright, wleft)
    for p in partners:
        pl.semaphore_signal(barrier, inc=1, device_id=p, device_id_type=MESH)
    pl.semaphore_wait(barrier, len(partners))

    g1 = send(w_in.at[:, cols(c)], wraw.at[z, c], zsame)
    g2 = send(w_in.at[:, cols(1 - c)], wraw.at[z, c], zother)
    g0 = send(w_in.at[:, cols(1 - c)], wraw.at[z, c], sib)

    def code_block(name, j):
        for copy in frag[name]:
            copy.wait()

        def body(i, carry):
            def at(g):
                return pl.ds(pl.multiple_of((i * (4 * SETS) + g) * 128, 128), 128)

            def delta_at(g):
                return anc[j, :, at(g)].astype(F32) - loc[j, :, at(g)].astype(F32)

            def store(g, value):
                cod[j, :, at(g)] = value

            code_chunk(delta_at, store)
            return carry

        lax.fori_loop(0, WC // (512 * SETS), body, 0)

    state = [{}, {}]

    def gather1(s):
        st = state[s]
        mine_a, mine_b = wa.at[s, y, xrows(x)], wb.at[s, y, xrows(x)]
        st["g1"] = (
            send(mine_a, mine_a, xright), send(mine_b, mine_b, yright),
            send(mine_a, mine_a, xleft), send(mine_b, mine_b, yleft),
        )

    def gather1_next(s):
        st = state[s]
        steps = (
            (wa.at[s, y, xrows_half(xl, 0)], xright), (wb.at[s, yl, xrows_half(x, 0)], yright),
            (wa.at[s, y, xrows_half(xr, 1)], xleft), (wb.at[s, yr, xrows_half(x, 1)], yleft),
        )
        out = []
        for copy, (ref, to) in zip(st["g1"], steps):
            arrived(copy)
            out.append(send(ref, ref, to))
        st["g2"] = out

    def gather2(s):
        st = state[s]
        a_r, b_r, a_l, b_l = st["g2"]
        arrived(a_r, a_l)
        mine_a, mine_b = wa.at[s, y], wb.at[s, :, xrows(x)]
        a_r, a_l = send(mine_a, mine_a, yright), send(mine_a, mine_a, yleft)
        arrived(b_r, b_l)
        b_r, b_l = send(mine_b, mine_b, xright), send(mine_b, mine_b, xleft)
        st["g3"] = (a_r, b_r, a_l, b_l)

    def gather2_next(s):
        st = state[s]
        steps = (
            (wa.at[s, yl, 0:hy], yright), (wb.at[s, 0:2, xrows(xl)], xright),
            (wa.at[s, yr, hy:YB], yleft), (wb.at[s, 2:4, xrows(xr)], xleft),
        )
        out = []
        for copy, (ref, to) in zip(st["g3"], steps):
            arrived(copy)
            out.append(send(ref, ref, to))
        st["g4"] = out

    def forward(s):
        arrived(*state[s]["g4"])

        def body(i, carry):
            t = i // 2
            r = pl.ds(pl.multiple_of(lax.rem(i, 2) * 256, 256), 256)
            weight = jnp.concatenate([wa[s].reshape(D, R), wb[s].reshape(D, R)], axis=1)
            value = jnp.dot(xs[t, r, :], weight, preferred_element_type=F32) * factor
            sig = jax.nn.sigmoid(value)
            cot = gs[t, r, 2 * R * s:2 * R * (s + 1)].astype(F32)
            act[s, t, r, :] = (cot * sig * (1.0 + value * (1.0 - sig))).astype(BF16)
            return carry

        lax.fori_loop(0, 4, body, 0)

    def backward(s, yy):
        at = pl.ds(pl.multiple_of(yy * YB, 128), YB)
        dims = (((0,), (0,)), ((), ()))
        part = lax.dot_general(xs[0, :, at], act[s, 0], dims, preferred_element_type=F32)
        part += lax.dot_general(xs[1, :, at], act[s, 1], dims, preferred_element_type=F32)
        pa[s, yy] = part[:, :R].astype(BF16)
        pb[s, yy] = part[:, R:].astype(BF16)

    def reduce1(s):
        st = state[s]
        backward(s, yo)
        a0 = send(pa.at[s, yo, 0:hy], ra_o.at[s, 0], yright)
        a1 = send(pa.at[s, yo, hy:YB], ra_o.at[s, 1], yleft)
        backward(s, yr)
        a2 = send(pa.at[s, yr, hy:YB], ra_l.at[s, hy:YB], yright)
        backward(s, yl)
        a3 = send(pa.at[s, yl, 0:hy], ra_r.at[s, 0:hy], yleft)
        backward(s, y)
        b0 = send(pb.at[s, 0:2, xrows(xo)], rb_o.at[s, 0], xright)
        b1 = send(pb.at[s, 2:4, xrows(xo)], rb_o.at[s, 1], xleft)
        b2 = send(pb.at[s, 2:4, xrows(xr)], rb_l.at[s, 2:4], xright)
        b3 = send(pb.at[s, 0:2, xrows(xl)], rb_r.at[s, 0:2], xleft)
        st["r1"] = (a0, a1, b0, b1)
        st["ra"], st["rb"] = [a2, a3], [b2, b3]

    def add_to(dst, at, other, n):
        def body(i, carry):
            r = pl.ds(pl.multiple_of(i * 96, 16), 96)
            d = pl.ds(pl.multiple_of(at + i * 96, 16), 96)
            dst[d, :] = (dst[d, :].astype(F32) + other[r, :].astype(F32)).astype(BF16)
            return carry

        lax.fori_loop(0, n // 96, body, 0)

    def reduce1_next(s):
        st = state[s]
        a0, a1, b0, b1 = st["r1"]
        arrived(a0)
        add_to(pa.at[s, yr], 0, ra_o.at[s, 0], hy)
        st["ra"].append(send(pa.at[s, yr, 0:hy], ra_l.at[s, 0:hy], yright))
        arrived(a1)
        add_to(pa.at[s, yl], hy, ra_o.at[s, 1], hy)
        st["ra"].append(send(pa.at[s, yl, hy:YB], ra_r.at[s, hy:YB], yleft))
        arrived(b0)
        for k in range(2):
            add_to(pb.at[s, k], xr * XB, rb_o.at[s, 0, k], XB)
        st["rb"].append(send(pb.at[s, 0:2, xrows(xr)], rb_l.at[s, 0:2], xright))
        arrived(b1)
        for k in range(2):
            add_to(pb.at[s, 2 + k], xl * XB, rb_o.at[s, 1, k], XB)
        st["rb"].append(send(pb.at[s, 2:4, xrows(xl)], rb_r.at[s, 2:4], xleft))

    def reduce2(s):
        st = state[s]
        arrived(*st["ra"])

        def sum_a(i, carry):
            r = pl.ds(pl.multiple_of(i * 192, 96), 192)
            total = pa[s, y, r, :].astype(F32) + ra_l[s, r, :].astype(F32) + ra_r[s, r, :].astype(F32)
            sa[s, r, :] = total
            sa16[s, r, :] = total.astype(BF16)
            return carry

        lax.fori_loop(0, YB // 192, sum_a, 0)
        a0 = send(sa16.at[s, xrows_half(xo, 0)], ta_o.at[s, 0], xright)
        a1 = send(sa16.at[s, xrows_half(xo, 1)], ta_o.at[s, 1], xleft)
        a2 = send(sa16.at[s, xrows_half(xr, 1)], ta_l.at[s, hx:XB], xright)
        a3 = send(sa16.at[s, xrows_half(xl, 0)], ta_r.at[s, 0:hx], xleft)

        arrived(*st["rb"])

        def sum_b(k, carry):
            total = pb[s, k, xrows(x), :].astype(F32) + rb_l[s, k].astype(F32) + rb_r[s, k].astype(F32)
            sb[s, k] = total
            sb16[s, k] = total.astype(BF16)
            return carry

        lax.fori_loop(0, 4, sum_b, 0)
        b0 = send(sb16.at[s, yo, 0:hx], tb_o.at[s, 0], yright)
        b1 = send(sb16.at[s, yo, hx:XB], tb_o.at[s, 1], yleft)
        b2 = send(sb16.at[s, yr, hx:XB], tb_l.at[s, hx:XB], yright)
        b3 = send(sb16.at[s, yl, 0:hx], tb_r.at[s, 0:hx], yleft)
        st["t1"] = (a0, a1, b0, b1)
        st["ta"], st["tb"] = [a2, a3], [b2, b3]

    def reduce2_next(s):
        st = state[s]
        a0, a1, b0, b1 = st["t1"]
        arrived(a0)
        r = xrows_half(xr, 0)
        sa16[s, r, :] = (sa[s, r, :] + ta_o[s, 0].astype(F32)).astype(BF16)
        st["ta"].append(send(sa16.at[s, r], ta_l.at[s, 0:hx], xright))
        arrived(a1)
        r = xrows_half(xl, 1)
        sa16[s, r, :] = (sa[s, r, :] + ta_o[s, 1].astype(F32)).astype(BF16)
        st["ta"].append(send(sa16.at[s, r], ta_r.at[s, hx:XB], xleft))
        arrived(b0)
        sb16[s, yr, 0:hx, :] = (sb[s, yr, 0:hx, :] + tb_o[s, 0].astype(F32)).astype(BF16)
        st["tb"].append(send(sb16.at[s, yr, 0:hx], tb_l.at[s, 0:hx], yright))
        arrived(b1)
        sb16[s, yl, hx:XB, :] = (sb[s, yl, hx:XB, :] + tb_o[s, 1].astype(F32)).astype(BF16)
        st["tb"].append(send(sb16.at[s, yl, hx:XB], tb_r.at[s, hx:XB], yleft))

    def part(zz, cc):
        return pl.ds(pl.multiple_of((zz * 2 + cc) * ROWS, 8), ROWS)

    def reduce3(s):
        st = state[s]
        arrived(*st["ta"])
        tt[s, :, 0:R] = sa[s, xrows(x), :] + ta_l[s].astype(F32) + ta_r[s].astype(F32)
        arrived(*st["tb"])
        tt[s, :, R:2 * R] = sb[s, y] + tb_l[s].astype(F32) + tb_r[s].astype(F32)
        for k in range(2):
            fz_send[s, k] = tt[s, part(1 - z, k), :].astype(BF16)
        f1 = send(fz_send.at[s, c], fz_recv.at[s, c], zsame)
        f2 = send(fz_send.at[s, 1 - c], fz_recv.at[s, c], zother)
        fs_send[s] = tt[s, part(z, 1 - c), :]
        f0 = send(fs_send.at[s], fs_recv.at[s], sib)
        st["f"] = (f1, f2, f0)

    def last(s):
        arrived(*state[s]["f"])

        def at(j):
            return pl.ds(pl.multiple_of(j * HALF + 2 * R * s, 2 * R), 2 * R)

        wg_v[:, at(c)] = (tt[s, part(z, c), :] + fz_recv[s, c].astype(F32)) * factor
        wg_v[:, at(1 - c)] = (fs_recv[s] + fz_recv[s, 1 - c].astype(F32)) * factor

    code_block("o", wo_i)
    w0 = send(half(cod.at[wo_i], 0), wo.at[0], wright)
    w1 = send(half(cod.at[wo_i], 1), wo.at[1], wleft)

    own_w.wait()
    arrived(g1, g2, g0)
    for zz in range(2):
        rows = jnp.concatenate(
            [wraw[zz, 0].astype(F32), wraw[zz, 1].astype(F32)], axis=0
        ).astype(BF16)
        for s in range(2):
            wa[s, y, xrows_half(x, zz), :] = rows[:, 2 * R * s:2 * R * s + R]
            wb[s, y, xrows_half(x, zz), :] = rows[:, 2 * R * s + R:2 * R * (s + 1)]

    gather1(0)
    sx = send(x_in, xs.at[1], sib)
    sg = send(g_in.at[:, cols(1 - c)], gs.at[1], sib)

    code_block("r", wr_i)
    w2 = send(half(cod.at[wr_i], 1), half(wl, 1), wright)
    gather1_next(0)
    gather1(1)
    code_block("l", wl_i)
    w3 = send(half(cod.at[wl_i], 0), half(wr, 0), wleft)
    gather2(0)
    gather1_next(1)
    code_block("s", wk)
    gather2_next(0)
    gather2(1)

    arrived(w0, w1)
    for j, h in ((wr_i, 0), (wl_i, 1)):
        def body(i, carry, j=j, h=h):
            at = pl.ds(pl.multiple_of(i * 256, 256), 256)
            to = pl.ds(pl.multiple_of(h * WH + i * 256, 256), 256)
            cod[j, :, to] = (cod[j, :, to].astype(F32) + wo[h, :, at].astype(F32)).astype(BF16)
            return carry
        lax.fori_loop(0, WH // 256, body, 0)
    w4 = send(half(cod.at[wr_i], 0), half(wl, 0), wright)
    w5 = send(half(cod.at[wl_i], 1), half(wr, 1), wleft)

    own_x.wait()
    own_g.wait()
    arrived(sx, sg)
    forward(0)
    gather2_next(1)
    reduce1(0)
    forward(1)
    reduce1_next(0)
    reduce1(1)
    reduce2(0)
    reduce1_next(1)

    arrived(w2, w3, w4, w5)
    own_m.wait()

    def outer(i, carry):
        at = pl.ds(pl.multiple_of(i * 256, 256), 256)
        total = cod[wk, :, at].astype(F32) + wl[:, at].astype(F32) + wr[:, at].astype(F32)
        grad = total * 0.25
        fresh = 0.9 * mom[:, at] + grad
        nm_v[:, at] = fresh
        na_v[:, at] = (anc[wk, :, at].astype(F32) - 0.7 * (grad + 0.9 * fresh)).astype(BF16)
        return carry

    lax.fori_loop(0, WC // 256, outer, 0)
    out1 = local(na_v, na_out)
    out2 = local(nm_v, nm_out)

    reduce2_next(0)
    reduce2(1)
    reduce3(0)
    reduce2_next(1)
    reduce3(1)
    last(0)
    last(1)
    out0 = local(wg_v, wg_out)
    for copy in pending:
        copy.wait_send()
    for copy in (out0, out1, out2):
        copy.wait()


def shards(inner_input, inner_weight, grad_out, local_fragment, anchor, momentum):
    any_spec = pl.BlockSpec(memory_space=pl.ANY)
    vm = pltpu.VMEM
    hy, hx = YB // 2, XB // 2
    wg, na, nm = pl.pallas_call(
        kernel,
        out_shape=(
            jax.ShapeDtypeStruct((ROWS, 1024), F32),
            jax.ShapeDtypeStruct((ROWS, WC), BF16),
            jax.ShapeDtypeStruct((ROWS, WC), F32),
        ),
        in_specs=[any_spec] * 6,
        out_specs=(any_spec,) * 3,
        scratch_shapes=[
            vm((2, TOK, D), BF16), vm((2, TOK, HALF), BF16), vm((2, 2, ROWS, HALF), BF16),
            vm((2, 4, YB, R), BF16), vm((2, 4, YB, R), BF16),
            vm((2, 2, TOK, 2 * R), BF16),
            vm((2, 4, YB, R), BF16), vm((2, 4, YB, R), BF16),
            vm((2, 2, hy, R), BF16), vm((2, YB, R), BF16), vm((2, YB, R), BF16),
            vm((2, 2, 2, XB, R), BF16), vm((2, 4, XB, R), BF16), vm((2, 4, XB, R), BF16),
            vm((2, YB, R), F32), vm((2, 4, XB, R), F32), vm((2, YB, R), BF16), vm((2, 4, XB, R), BF16),
            vm((2, 2, hx, R), BF16), vm((2, XB, R), BF16), vm((2, XB, R), BF16),
            vm((2, 2, hx, R), BF16), vm((2, XB, R), BF16), vm((2, XB, R), BF16),
            vm((2, XB, 2 * R), F32),
            vm((2, ROWS, 2 * R), F32), vm((2, ROWS, 2 * R), F32),
            vm((2, 2, ROWS, 2 * R), BF16), vm((2, 2, ROWS, 2 * R), BF16),
            vm((ROWS, 1024), F32),
            vm((4, ROWS, WC), BF16), vm((4, ROWS, WC), BF16), vm((ROWS, WC), F32),
            vm((4, ROWS, WC), BF16),
            vm((2, ROWS, WH), BF16), vm((ROWS, WC), BF16), vm((ROWS, WC), BF16),
            vm((ROWS, WC), BF16), vm((ROWS, WC), F32),
            pltpu.SemaphoreType.DMA((16,)),
            pltpu.SemaphoreType.DMA((100,)),
            pltpu.SemaphoreType.DMA((100,)),
        ],
        compiler_params=pltpu.CompilerParams(
            collective_id=0, has_side_effects=True, vmem_limit_bytes=60 * 1024 * 1024
        ),
        cost_estimate=pl.CostEstimate(
            flops=4 * TOK * D * 1024, bytes_accessed=16 * 1024 * 1024, transcendentals=TOK * 1024
        ),
    )(inner_input[0], inner_weight[0], grad_out[0], local_fragment[0], anchor, momentum)
    return (wg[None], na, nm)


def solution(mesh):
    in_specs = (
        P("worker", "fsdp", None),
        P("worker", "fsdp", None),
        P("worker", "fsdp", None),
        P("worker", "fsdp", None),
        P("fsdp", None),
        P("fsdp", "worker"),
    )
    out_specs = (P("worker", "fsdp", None), P("fsdp", "worker"), P("fsdp", "worker"))
    return jax.shard_map(shards, mesh=mesh, in_specs=in_specs, out_specs=out_specs, check_vma=False)
```

time: 95.9 us -> 94.2 us (0.982)
  the two profiles are of different devices: /device:TPU:1 before, /device:TPU:72 now
where the time goes in v3:
time: 94.2 us; the launch traced here: 94.1 us
  Pallas kernels  88.6 us (94%)
  local copies, waits for them, and re-layouts  4.83 us (5%)
    pallas_call x1, Pallas kernels, shards(): pl.pallas_call(kernel, out_shape=(jax.ShapeDtypeStruct((ROWS, 1024), F32)...  88.6 us
    unnamed x5, local copies, waits for them, and re-layouts  4.83 us

profile of v3, /device:TPU:72, one launch (start us, length us, event | category | flops | bytes accessed | tf_op | source)
XLA Modules:
  0.0 94.1 jit_solution(10973131107870778198)
XLA Ops:
  0.6 88.6 %shard_map.85 = (f32[72,1024]{1,0:T(8,128)}, bf16[72,4608]{1,0:T(8,128)(2,1)}, f32[72,4608]{1,0:T(8,128)}) custom-call(bf16[512,4608]{1,0:T(8,128)(2,1)} %bitcast.6, bf16[72,1024]{1,0:T(8,128)(2,1)} %bitcast.9, bf16[512,1024]{1,0:T(8,128)(2,1)} %bitcast.8, bf16[72,18432]{1,0:T(8,128)(2,1)} %bitcast.7, bf16[72,18432]{1,0:T(8,128)(2,1)} %anc_in.1, ...), custom_call_target="tpu_custom_call" | custom-call | flops 9663676416 | bytes 16777216 | tf_op jit(solution)/shard_map/pallas_call | solution.py:464
  89.3 0.0 copy-start
  89.3 1.8 %copy.12 = f32[1,72,1024]{2,1,0:T(8,128)} copy(f32[1,72,1024]{2,1,0:T(8,128)} %bitcast.5) | data formatting | bytes 589824
  91.1 2.0 %copy.13 = bf16[72,4608]{1,0:T(8,128)(2,1)} copy(bf16[72,4608]{1,0:T(8,128)(2,1)} %get-tuple-element.13) | data formatting | bytes 1327104
  93.0 0.0 copy-done
  93.0 1.1 %copy.14 = f32[72,4608]{1,0:T(8,128)} copy(f32[72,4608]{1,0:T(8,128)S(1)} %copy-done) | data formatting | bytes 2654208
Async XLA Ops:
  89.3 3.8 %copy-start = (f32[72,4608]{1,0:T(8,128)S(1)}, f32[72,4608]{1,0:T(8,128)}, u32[]{:S(2)}) copy-start(f32[72,4608]{1,0:T(8,128)} %get-tuple-element.14) | copy-start | bytes 3981316

commit v4 on v3

--- a/solution.py
+++ b/solution.py
@@ -80,7 +80,7 @@
     xs, gs, wraw, wa, wb, act, pa, pb,
     ra_o, ra_l, ra_r, rb_o, rb_l, rb_r,
     sa, sb, sa16, sb16,
-    ta_o, ta_l, ta_r, tb_o, tb_l, tb_r,
+    ta, tb,
     tt, fs_send, fs_recv, fz_send, fz_recv, wg_v,
     loc, anc, mom, cod, wo, wl, wr, na_v, nm_v,
     lsem, ssem, rsem,
@@ -105,6 +105,7 @@
     zother = dev(y, x, 1 - z, 1 - c)
     xright, xleft = dev(y, xr, z, c), dev(y, xl, z, c)
     yright, yleft = dev(yr, x, z, c), dev(yl, x, z, c)
+    xopp, yopp = dev(y, xo, z, c), dev(yo, x, z, c)
     wright, wleft = (wr_i, me), (wl_i, me)
 
     pending = []
@@ -158,7 +159,7 @@
     own_m = local(mom_in, mom)
 
     barrier = pltpu.get_barrier_semaphore()
-    partners = (sib, zsame, zother, xright, xleft, yright, yleft, wright, wleft)
+    partners = (sib, zsame, zother, xright, xleft, xopp, yright, yleft, yopp, wright, wleft)
     for p in partners:
         pl.semaphore_signal(barrier, inc=1, device_id=p, device_id_type=MESH)
     pl.semaphore_wait(barrier, len(partners))
@@ -189,34 +190,26 @@
     state = [{}, {}]
 
     def gather1(s):
-        st = state[s]
         mine_a, mine_b = wa.at[s, y, xrows(x)], wb.at[s, y, xrows(x)]
-        st["g1"] = (
-            send(mine_a, mine_a, xright), send(mine_b, mine_b, yright),
-            send(mine_a, mine_a, xleft), send(mine_b, mine_b, yleft),
-        )
-
-    def gather1_next(s):
-        st = state[s]
-        steps = (
-            (wa.at[s, y, xrows_half(xl, 0)], xright), (wb.at[s, yl, xrows_half(x, 0)], yright),
-            (wa.at[s, y, xrows_half(xr, 1)], xleft), (wb.at[s, yr, xrows_half(x, 1)], yleft),
-        )
         out = []
-        for copy, (ref, to) in zip(st["g1"], steps):
-            arrived(copy)
-            out.append(send(ref, ref, to))
-        st["g2"] = out
+        for a_to, b_to in ((xright, yright), (xleft, yleft), (xopp, yopp)):
+            out.append(send(mine_a, mine_a, a_to))
+            out.append(send(mine_b, mine_b, b_to))
+        state[s]["g1"] = out
 
     def gather2(s):
         st = state[s]
-        a_r, b_r, a_l, b_l = st["g2"]
-        arrived(a_r, a_l)
-        mine_a, mine_b = wa.at[s, y], wb.at[s, :, xrows(x)]
-        a_r, a_l = send(mine_a, mine_a, yright), send(mine_a, mine_a, yleft)
-        arrived(b_r, b_l)
-        b_r, b_l = send(mine_b, mine_b, xright), send(mine_b, mine_b, xleft)
-        st["g3"] = (a_r, b_r, a_l, b_l)
+        arrived(*st["g1"])
+        a = (wa.at[s, y, 0:hy], wa.at[s, y, hy:YB])
+        b = (wb.at[s, 0:2, xrows(x)], wb.at[s, 2:4, xrows(x)])
+        st["g2"] = (
+            send(a[0], a[0], yright), send(b[0], b[0], xright),
+            send(a[1], a[1], yleft), send(b[1], b[1], xleft),
+        )
+        st["g3"] = [
+            send(a[1], a[1], yright), send(b[1], b[1], xright),
+            send(a[0], a[0], yleft), send(b[0], b[0], xleft),
+        ]
 
     def gather2_next(s):
         st = state[s]
@@ -224,14 +217,12 @@
             (wa.at[s, yl, 0:hy], yright), (wb.at[s, 0:2, xrows(xl)], xright),
             (wa.at[s, yr, hy:YB], yleft), (wb.at[s, 2:4, xrows(xr)], xleft),
         )
-        out = []
-        for copy, (ref, to) in zip(st["g3"], steps):
+        for copy, (ref, to) in zip(st["g2"], steps):
             arrived(copy)
-            out.append(send(ref, ref, to))
-        st["g4"] = out
+            st["g3"].append(send(ref, ref, to))
 
     def forward(s):
-        arrived(*state[s]["g4"])
+        arrived(*state[s]["g3"])
 
         def body(i, carry):
             t = i // 2
@@ -309,11 +300,10 @@
             return carry
 
         lax.fori_loop(0, YB // 192, sum_a, 0)
-        a0 = send(sa16.at[s, xrows_half(xo, 0)], ta_o.at[s, 0], xright)
-        a1 = send(sa16.at[s, xrows_half(xo, 1)], ta_o.at[s, 1], xleft)
-        a2 = send(sa16.at[s, xrows_half(xr, 1)], ta_l.at[s, hx:XB], xright)
-        a3 = send(sa16.at[s, xrows_half(xl, 0)], ta_r.at[s, 0:hx], xleft)
-
+        st["ta"] = [
+            send(sa16.at[s, xrows(j)], ta.at[s, k], to)
+            for k, (j, to) in enumerate(((xo, xopp), (xr, xright), (xl, xleft)))
+        ]
         arrived(*st["rb"])
 
         def sum_b(k, carry):
@@ -323,30 +313,10 @@
             return carry
 
         lax.fori_loop(0, 4, sum_b, 0)
-        b0 = send(sb16.at[s, yo, 0:hx], tb_o.at[s, 0], yright)
-        b1 = send(sb16.at[s, yo, hx:XB], tb_o.at[s, 1], yleft)
-        b2 = send(sb16.at[s, yr, hx:XB], tb_l.at[s, hx:XB], yright)
-        b3 = send(sb16.at[s, yl, 0:hx], tb_r.at[s, 0:hx], yleft)
-        st["t1"] = (a0, a1, b0, b1)
-        st["ta"], st["tb"] = [a2, a3], [b2, b3]
-
-    def reduce2_next(s):
-        st = state[s]
-        a0, a1, b0, b1 = st["t1"]
-        arrived(a0)
-        r = xrows_half(xr, 0)
-        sa16[s, r, :] = (sa[s, r, :] + ta_o[s, 0].astype(F32)).astype(BF16)
-        st["ta"].append(send(sa16.at[s, r], ta_l.at[s, 0:hx], xright))
-        arrived(a1)
-        r = xrows_half(xl, 1)
-        sa16[s, r, :] = (sa[s, r, :] + ta_o[s, 1].astype(F32)).astype(BF16)
-        st["ta"].append(send(sa16.at[s, r], ta_r.at[s, hx:XB], xleft))
-        arrived(b0)
-        sb16[s, yr, 0:hx, :] = (sb[s, yr, 0:hx, :] + tb_o[s, 0].astype(F32)).astype(BF16)
-        st["tb"].append(send(sb16.at[s, yr, 0:hx], tb_l.at[s, 0:hx], yright))
-        arrived(b1)
-        sb16[s, yl, hx:XB, :] = (sb[s, yl, hx:XB, :] + tb_o[s, 1].astype(F32)).astype(BF16)
-        st["tb"].append(send(sb16.at[s, yl, hx:XB], tb_r.at[s, hx:XB], yleft))
+        st["tb"] = [
+            send(sb16.at[s, j], tb.at[s, k], to)
+            for k, (j, to) in enumerate(((yo, yopp), (yr, yright), (yl, yleft)))
+        ]
 
     def part(zz, cc):
         return pl.ds(pl.multiple_of((zz * 2 + cc) * ROWS, 8), ROWS)
@@ -354,9 +324,13 @@
     def reduce3(s):
         st = state[s]
         arrived(*st["ta"])
-        tt[s, :, 0:R] = sa[s, xrows(x), :] + ta_l[s].astype(F32) + ta_r[s].astype(F32)
+        tt[s, :, 0:R] = sa[s, xrows(x), :] + (
+            ta[s, 0].astype(F32) + ta[s, 1].astype(F32) + ta[s, 2].astype(F32)
+        )
         arrived(*st["tb"])
-        tt[s, :, R:2 * R] = sb[s, y] + tb_l[s].astype(F32) + tb_r[s].astype(F32)
+        tt[s, :, R:2 * R] = sb[s, y] + (
+            tb[s, 0].astype(F32) + tb[s, 1].astype(F32) + tb[s, 2].astype(F32)
+        )
         for k in range(2):
             fz_send[s, k] = tt[s, part(1 - z, k), :].astype(BF16)
         f1 = send(fz_send.at[s, c], fz_recv.at[s, c], zsame)
@@ -389,20 +363,24 @@
             wb[s, y, xrows_half(x, zz), :] = rows[:, 2 * R * s + R:2 * R * (s + 1)]
 
     gather1(0)
+    gather1(1)
     sx = send(x_in, xs.at[1], sib)
     sg = send(g_in.at[:, cols(1 - c)], gs.at[1], sib)
 
     code_block("r", wr_i)
     w2 = send(half(cod.at[wr_i], 1), half(wl, 1), wright)
-    gather1_next(0)
-    gather1(1)
+    gather2(0)
     code_block("l", wl_i)
     w3 = send(half(cod.at[wl_i], 0), half(wr, 0), wleft)
-    gather2(0)
-    gather1_next(1)
-    code_block("s", wk)
     gather2_next(0)
     gather2(1)
+    code_block("s", wk)
+    gather2_next(1)
+
+    own_x.wait()
+    own_g.wait()
+    arrived(sx, sg)
+    forward(0)
 
     arrived(w0, w1)
     for j, h in ((wr_i, 0), (wl_i, 1)):
@@ -415,11 +393,6 @@
     w4 = send(half(cod.at[wr_i], 0), half(wl, 0), wright)
     w5 = send(half(cod.at[wl_i], 1), half(wr, 1), wleft)
 
-    own_x.wait()
-    own_g.wait()
-    arrived(sx, sg)
-    forward(0)
-    gather2_next(1)
     reduce1(0)
     forward(1)
     reduce1_next(0)
@@ -443,10 +416,8 @@
     out1 = local(na_v, na_out)
     out2 = local(nm_v, nm_out)
 
-    reduce2_next(0)
+    reduce3(0)
     reduce2(1)
-    reduce3(0)
-    reduce2_next(1)
     reduce3(1)
     last(0)
     last(1)
@@ -454,6 +425,17 @@
     for copy in pending:
         copy.wait_send()
     for copy in (out0, out1, out2):
+        copy.wait()
+
+
+def hand_on(wg_in, na_in, nm_in, wg_out, na_out, nm_out, sem):
+    copies = [
+        pltpu.make_async_copy(src, dst, sem.at[k])
+        for k, (src, dst) in enumerate(((nm_in, nm_out), (na_in, na_out), (wg_in, wg_out)))
+    ]
+    for copy in copies:
+        copy.start()
+    for copy in copies:
         copy.wait()
 
 
@@ -478,8 +460,7 @@
             vm((2, 2, hy, R), BF16), vm((2, YB, R), BF16), vm((2, YB, R), BF16),
             vm((2, 2, 2, XB, R), BF16), vm((2, 4, XB, R), BF16), vm((2, 4, XB, R), BF16),
             vm((2, YB, R), F32), vm((2, 4, XB, R), F32), vm((2, YB, R), BF16), vm((2, 4, XB, R), BF16),
-            vm((2, 2, hx, R), BF16), vm((2, XB, R), BF16), vm((2, XB, R), BF16),
-            vm((2, 2, hx, R), BF16), vm((2, XB, R), BF16), vm((2, XB, R), BF16),
+            vm((2, 3, XB, R), BF16), vm((2, 3, XB, R), BF16),
             vm((2, XB, 2 * R), F32),
             vm((2, ROWS, 2 * R), F32), vm((2, ROWS, 2 * R), F32),
             vm((2, 2, ROWS, 2 * R), BF16), vm((2, 2, ROWS, 2 * R), BF16),
@@ -499,6 +480,13 @@
             flops=4 * TOK * D * 1024, bytes_accessed=16 * 1024 * 1024, transcendentals=TOK * 1024
         ),
     )(inner_input[0], inner_weight[0], grad_out[0], local_fragment[0], anchor, momentum)
+    wg, na, nm = pl.pallas_call(
+        hand_on,
+        out_shape=tuple(jax.ShapeDtypeStruct(a.shape, a.dtype) for a in (wg, na, nm)),
+        in_specs=[any_spec] * 3,
+        out_specs=(any_spec,) * 3,
+        scratch_shapes=[pltpu.SemaphoreType.DMA((3,))],
+    )(wg, na, nm)
     return (wg[None], na, nm)
 
 

time: 94.2 us -> 156 us (1.66)
  the two profiles are of different devices: /device:TPU:72 before, /device:TPU:64 now
where the time goes in v4:
time: 156 us
  Pallas kernels  155 us (99%)
    pallas_call x1, Pallas kernels, shards(): pl.pallas_call(kernel, out_shape=(jax.ShapeDtypeStruct((ROWS, 1024), F32)...  84.3 us
    pallas_call x1, Pallas kernels, shards(): pl.pallas_call(hand_on, out_shape=tuple((jax.ShapeDtypeStruct(a.shape, a....  70.4 us

profile of v4, /device:TPU:64, one launch (start us, length us, event | category | flops | bytes accessed | tf_op | source)
XLA Modules:
  0.0 155.5 jit_solution(18257049463464934444)
XLA Ops:
  0.6 84.3 %shard_map.85 = (f32[72,1024]{1,0:T(8,128)}, bf16[72,4608]{1,0:T(8,128)(2,1)}, f32[72,4608]{1,0:T(8,128)}) custom-call(bf16[512,4608]{1,0:T(8,128)(2,1)} %bitcast.5, bf16[72,1024]{1,0:T(8,128)(2,1)} %bitcast.9, bf16[512,1024]{1,0:T(8,128)(2,1)} %bitcast.7, bf16[72,18432]{1,0:T(8,128)(2,1)} %bitcast.6, bf16[72,18432]{1,0:T(8,128)(2,1)} %anc_in.1, ...), custom_call_target="tpu_custom_call" | custom-call | flops 9663676416 | bytes 16777216 | tf_op jit(solution)/shard_map/pallas_call | solution.py:446
  85.0 70.4 %shard_map.86 = (f32[72,1024]{1,0:T(8,128)}, bf16[72,4608]{1,0:T(8,128)(2,1)}, f32[72,4608]{1,0:T(8,128)}) custom-call(f32[72,1024]{1,0:T(8,128)} %get-tuple-element.9.wg_in, bf16[72,4608]{1,0:T(8,128)(2,1)} %get-tuple-element.10.na_in, f32[72,4608]{1,0:T(8,128)} %get-tuple-element.11.nm_in), custom_call_target="tpu_custom_call" | custom-call | tf_op jit(solution)/shard_map/pallas_call | solution.py:483

commit v5 on v4

--- a/solution.py
+++ b/solution.py
@@ -428,14 +428,16 @@
         copy.wait()
 
 
-def hand_on(wg_in, na_in, nm_in, wg_out, na_out, nm_out, sem):
-    copies = [
-        pltpu.make_async_copy(src, dst, sem.at[k])
-        for k, (src, dst) in enumerate(((nm_in, nm_out), (na_in, na_out), (wg_in, wg_out)))
-    ]
-    for copy in copies:
+def hand_on(wg_in, na_in, nm_in, wg_out, na_out, nm_out, wg_v, na_v, nm_v, sem):
+    arrays = ((nm_in, nm_v, nm_out), (na_in, na_v, na_out), (wg_in, wg_v, wg_out))
+    reads = [pltpu.make_async_copy(a, v, sem.at[0, k]) for k, (a, v, b) in enumerate(arrays)]
+    writes = [pltpu.make_async_copy(v, b, sem.at[1, k]) for k, (a, v, b) in enumerate(arrays)]
+    for copy in reads:
         copy.start()
-    for copy in copies:
+    for read, write in zip(reads, writes):
+        read.wait()
+        write.start()
+    for copy in writes:
         copy.wait()
 
 
@@ -485,7 +487,7 @@
         out_shape=tuple(jax.ShapeDtypeStruct(a.shape, a.dtype) for a in (wg, na, nm)),
         in_specs=[any_spec] * 3,
         out_specs=(any_spec,) * 3,
-        scratch_shapes=[pltpu.SemaphoreType.DMA((3,))],
+        scratch_shapes=[vm(a.shape, a.dtype) for a in (wg, na, nm)] + [pltpu.SemaphoreType.DMA((2, 3))],
     )(wg, na, nm)
     return (wg[None], na, nm)
 

time: 156 us -> 88 us (0.56)
  Pallas kernels: 155 us -> 87.1 us
    pallas_call x1, Pallas kernels: 70.4 us -> 2.74 us  [shards(): pl.pallas_call(hand_on, out_shape=tuple((jax.ShapeDtypeStruct(a.shape, a....]
where the time goes in v5:
time: 88 us; the launch traced here: 87.9 us
  Pallas kernels  87.1 us (99%)
    pallas_call x1, Pallas kernels, shards(): pl.pallas_call(kernel, out_shape=(jax.ShapeDtypeStruct((ROWS, 1024), F32)...  84.3 us
    pallas_call x1, Pallas kernels, shards(): pl.pallas_call(hand_on, out_shape=tuple((jax.ShapeDtypeStruct(a.shape, a....  2.74 us

profile of v5, /device:TPU:64, one launch (start us, length us, event | category | flops | bytes accessed | tf_op | source)
XLA Modules:
  0.0 87.9 jit_solution(16686852479966728214)
XLA Ops:
  0.6 84.3 %shard_map.85 = (f32[72,1024]{1,0:T(8,128)}, bf16[72,4608]{1,0:T(8,128)(2,1)}, f32[72,4608]{1,0:T(8,128)}) custom-call(bf16[512,4608]{1,0:T(8,128)(2,1)} %bitcast.5, bf16[72,1024]{1,0:T(8,128)(2,1)} %bitcast.9, bf16[512,1024]{1,0:T(8,128)(2,1)} %bitcast.7, bf16[72,18432]{1,0:T(8,128)(2,1)} %bitcast.6, bf16[72,18432]{1,0:T(8,128)(2,1)} %anc_in.1, ...), custom_call_target="tpu_custom_call" | custom-call | flops 9663676416 | bytes 16777216 | tf_op jit(solution)/shard_map/pallas_call | solution.py:448
  85.0 2.7 %shard_map.86 = (f32[72,1024]{1,0:T(8,128)}, bf16[72,4608]{1,0:T(8,128)(2,1)}, f32[72,4608]{1,0:T(8,128)}) custom-call(f32[72,1024]{1,0:T(8,128)} %get-tuple-element.9.wg_in, bf16[72,4608]{1,0:T(8,128)(2,1)} %get-tuple-element.10.na_in, f32[72,4608]{1,0:T(8,128)} %get-tuple-element.11.nm_in), custom_call_target="tpu_custom_call" | custom-call | tf_op jit(solution)/shard_map/pallas_call | solution.py:485

commit v6 on v5

--- a/solution.py
+++ b/solution.py
@@ -221,12 +221,12 @@
             arrived(copy)
             st["g3"].append(send(ref, ref, to))
 
-    def forward(s):
-        arrived(*state[s]["g3"])
+    def forward(s, t):
+        if t == 0:
+            arrived(*state[s]["g3"])
 
         def body(i, carry):
-            t = i // 2
-            r = pl.ds(pl.multiple_of(lax.rem(i, 2) * 256, 256), 256)
+            r = pl.ds(pl.multiple_of(i * 256, 256), 256)
             weight = jnp.concatenate([wa[s].reshape(D, R), wb[s].reshape(D, R)], axis=1)
             value = jnp.dot(xs[t, r, :], weight, preferred_element_type=F32) * factor
             sig = jax.nn.sigmoid(value)
@@ -234,30 +234,30 @@
             act[s, t, r, :] = (cot * sig * (1.0 + value * (1.0 - sig))).astype(BF16)
             return carry
 
-        lax.fori_loop(0, 4, body, 0)
-
-    def backward(s, yy):
+        lax.fori_loop(0, 2, body, 0)
+
+    def backward(s, yy, slot):
         at = pl.ds(pl.multiple_of(yy * YB, 128), YB)
         dims = (((0,), (0,)), ((), ()))
         part = lax.dot_general(xs[0, :, at], act[s, 0], dims, preferred_element_type=F32)
         part += lax.dot_general(xs[1, :, at], act[s, 1], dims, preferred_element_type=F32)
         pa[s, yy] = part[:, :R].astype(BF16)
-        pb[s, yy] = part[:, R:].astype(BF16)
+        pb[s, slot] = part[:, R:].astype(BF16)
 
     def reduce1(s):
         st = state[s]
-        backward(s, yo)
+        backward(s, yo, 0)
         a0 = send(pa.at[s, yo, 0:hy], ra_o.at[s, 0], yright)
         a1 = send(pa.at[s, yo, hy:YB], ra_o.at[s, 1], yleft)
-        backward(s, yr)
+        backward(s, yr, 1)
+        b0 = send(pb.at[s, 0:2, xrows(xo)], rb_o.at[s, 0], xright)
+        b3 = send(pb.at[s, 0:2, xrows(xl)], rb_r.at[s, 0:2], xleft)
         a2 = send(pa.at[s, yr, hy:YB], ra_l.at[s, hy:YB], yright)
-        backward(s, yl)
+        backward(s, yl, 2)
         a3 = send(pa.at[s, yl, 0:hy], ra_r.at[s, 0:hy], yleft)
-        backward(s, y)
-        b0 = send(pb.at[s, 0:2, xrows(xo)], rb_o.at[s, 0], xright)
+        backward(s, y, 3)
         b1 = send(pb.at[s, 2:4, xrows(xo)], rb_o.at[s, 1], xleft)
         b2 = send(pb.at[s, 2:4, xrows(xr)], rb_l.at[s, 2:4], xright)
-        b3 = send(pb.at[s, 0:2, xrows(xl)], rb_r.at[s, 0:2], xleft)
         st["r1"] = (a0, a1, b0, b1)
         st["ra"], st["rb"] = [a2, a3], [b2, b3]
 
@@ -314,8 +314,7 @@
 
         lax.fori_loop(0, 4, sum_b, 0)
         st["tb"] = [
-            send(sb16.at[s, j], tb.at[s, k], to)
-            for k, (j, to) in enumerate(((yo, yopp), (yr, yright), (yl, yleft)))
+            send(sb16.at[s, k], tb.at[s, k], to) for k, to in enumerate((yopp, yright, yleft))
         ]
 
     def part(zz, cc):
@@ -328,7 +327,7 @@
             ta[s, 0].astype(F32) + ta[s, 1].astype(F32) + ta[s, 2].astype(F32)
         )
         arrived(*st["tb"])
-        tt[s, :, R:2 * R] = sb[s, y] + (
+        tt[s, :, R:2 * R] = sb[s, 3] + (
             tb[s, 0].astype(F32) + tb[s, 1].astype(F32) + tb[s, 2].astype(F32)
         )
         for k in range(2):
@@ -349,8 +348,6 @@
         wg_v[:, at(1 - c)] = (fs_recv[s] + fz_recv[s, 1 - c].astype(F32)) * factor
 
     code_block("o", wo_i)
-    w0 = send(half(cod.at[wo_i], 0), wo.at[0], wright)
-    w1 = send(half(cod.at[wo_i], 1), wo.at[1], wleft)
 
     own_w.wait()
     arrived(g1, g2, g0)
@@ -364,6 +361,8 @@
 
     gather1(0)
     gather1(1)
+    w0 = send(half(cod.at[wo_i], 0), wo.at[0], wright)
+    w1 = send(half(cod.at[wo_i], 1), wo.at[1], wleft)
     sx = send(x_in, xs.at[1], sib)
     sg = send(g_in.at[:, cols(1 - c)], gs.at[1], sib)
 
@@ -375,12 +374,14 @@
     gather2_next(0)
     gather2(1)
     code_block("s", wk)
-    gather2_next(1)
 
     own_x.wait()
     own_g.wait()
     arrived(sx, sg)
-    forward(0)
+    forward(0, 0)
+    gather2_next(1)
+    forward(0, 1)
+    reduce1(0)
 
     arrived(w0, w1)
     for j, h in ((wr_i, 0), (wl_i, 1)):
@@ -393,8 +394,8 @@
     w4 = send(half(cod.at[wr_i], 0), half(wl, 0), wright)
     w5 = send(half(cod.at[wl_i], 1), half(wr, 1), wleft)
 
-    reduce1(0)
-    forward(1)
+    forward(1, 0)
+    forward(1, 1)
     reduce1_next(0)
     reduce1(1)
     reduce2(0)

time: 88 us -> 83.4 us (0.948)
  the two profiles are of different devices: /device:TPU:64 before, /device:TPU:1 now
where the time goes in v6:
time: 83.4 us; the launch traced here: 83.3 us
  Pallas kernels  82.5 us (99%)
    pallas_call x1, Pallas kernels, shards(): pl.pallas_call(kernel, out_shape=(jax.ShapeDtypeStruct((ROWS, 1024), F32)...  79.7 us
    pallas_call x1, Pallas kernels, shards(): pl.pallas_call(hand_on, out_shape=tuple((jax.ShapeDtypeStruct(a.shape, a....  2.74 us

profile of v6, /device:TPU:1, one launch (start us, length us, event | category | flops | bytes accessed | tf_op | source)
XLA Modules:
  0.0 83.3 jit_solution(15133705527267312400)
XLA Ops:
  0.6 79.7 %shard_map.85 = (f32[72,1024]{1,0:T(8,128)}, bf16[72,4608]{1,0:T(8,128)(2,1)}, f32[72,4608]{1,0:T(8,128)}) custom-call(bf16[512,4608]{1,0:T(8,128)(2,1)} %bitcast.5, bf16[72,1024]{1,0:T(8,128)(2,1)} %bitcast.9, bf16[512,1024]{1,0:T(8,128)(2,1)} %bitcast.7, bf16[72,18432]{1,0:T(8,128)(2,1)} %bitcast.6, bf16[72,18432]{1,0:T(8,128)(2,1)} %anc_in.1, ...), custom_call_target="tpu_custom_call" | custom-call | flops 9663676416 | bytes 16777216 | tf_op jit(solution)/shard_map/pallas_call | solution.py:449
  80.4 2.7 %shard_map.86 = (f32[72,1024]{1,0:T(8,128)}, bf16[72,4608]{1,0:T(8,128)(2,1)}, f32[72,4608]{1,0:T(8,128)}) custom-call(f32[72,1024]{1,0:T(8,128)} %get-tuple-element.9.wg_in, bf16[72,4608]{1,0:T(8,128)(2,1)} %get-tuple-element.10.na_in, f32[72,4608]{1,0:T(8,128)} %get-tuple-element.11.nm_in), custom_call_target="tpu_custom_call" | custom-call | tf_op jit(solution)/shard_map/pallas_call | solution.py:486

commit v7 on v6

--- a/solution.py
+++ b/solution.py
@@ -417,8 +417,8 @@
     out1 = local(na_v, na_out)
     out2 = local(nm_v, nm_out)
 
+    reduce2(1)
     reduce3(0)
-    reduce2(1)
     reduce3(1)
     last(0)
     last(1)
@@ -430,9 +430,14 @@
 
 
 def hand_on(wg_in, na_in, nm_in, wg_out, na_out, nm_out, wg_v, na_v, nm_v, sem):
-    arrays = ((nm_in, nm_v, nm_out), (na_in, na_v, na_out), (wg_in, wg_v, wg_out))
-    reads = [pltpu.make_async_copy(a, v, sem.at[0, k]) for k, (a, v, b) in enumerate(arrays)]
-    writes = [pltpu.make_async_copy(v, b, sem.at[1, k]) for k, (a, v, b) in enumerate(arrays)]
+    h = WC // 4
+    parts = [
+        (a.at[:, k * h:(k + 1) * h], v.at[:, k * h:(k + 1) * h], b.at[:, k * h:(k + 1) * h])
+        for a, v, b in ((nm_in, nm_v, nm_out), (na_in, na_v, na_out))
+        for k in range(4)
+    ] + [(wg_in, wg_v, wg_out)]
+    reads = [pltpu.make_async_copy(a, v, sem.at[0, k]) for k, (a, v, b) in enumerate(parts)]
+    writes = [pltpu.make_async_copy(v, b, sem.at[1, k]) for k, (a, v, b) in enumerate(parts)]
     for copy in reads:
         copy.start()
     for read, write in zip(reads, writes):
@@ -488,7 +493,7 @@
         out_shape=tuple(jax.ShapeDtypeStruct(a.shape, a.dtype) for a in (wg, na, nm)),
         in_specs=[any_spec] * 3,
         out_specs=(any_spec,) * 3,
-        scratch_shapes=[vm(a.shape, a.dtype) for a in (wg, na, nm)] + [pltpu.SemaphoreType.DMA((2, 3))],
+        scratch_shapes=[vm(a.shape, a.dtype) for a in (wg, na, nm)] + [pltpu.SemaphoreType.DMA((2, 9))],
     )(wg, na, nm)
     return (wg[None], na, nm)
 

time: 83.4 us -> 83.1 us (level)
  no operation moved by 1% of the time
where the time goes in v7:
time: 83.1 us; the launch traced here: 83 us
  Pallas kernels  82.2 us (99%)
    pallas_call x1, Pallas kernels, shards(): pl.pallas_call(kernel, out_shape=(jax.ShapeDtypeStruct((ROWS, 1024), F32)...  79.7 us
    pallas_call x1, Pallas kernels, shards(): pl.pallas_call(hand_on, out_shape=tuple((jax.ShapeDtypeStruct(a.shape, a....  2.5 us

profile of v7, /device:TPU:1, one launch (start us, length us, event | category | flops | bytes accessed | tf_op | source)
XLA Modules:
  0.0 83.0 jit_solution(16056735266150857036)
XLA Ops:
  0.6 79.7 %shard_map.85 = (f32[72,1024]{1,0:T(8,128)}, bf16[72,4608]{1,0:T(8,128)(2,1)}, f32[72,4608]{1,0:T(8,128)}) custom-call(bf16[512,4608]{1,0:T(8,128)(2,1)} %bitcast.5, bf16[72,1024]{1,0:T(8,128)(2,1)} %bitcast.9, bf16[512,1024]{1,0:T(8,128)(2,1)} %bitcast.7, bf16[72,18432]{1,0:T(8,128)(2,1)} %bitcast.6, bf16[72,18432]{1,0:T(8,128)(2,1)} %anc_in.1, ...), custom_call_target="tpu_custom_call" | custom-call | flops 9663676416 | bytes 16777216 | tf_op jit(solution)/shard_map/pallas_call | solution.py:454
  80.4 2.5 %shard_map.86 = (f32[72,1024]{1,0:T(8,128)}, bf16[72,4608]{1,0:T(8,128)(2,1)}, f32[72,4608]{1,0:T(8,128)}) custom-call(f32[72,1024]{1,0:T(8,128)} %get-tuple-element.9.wg_in, bf16[72,4608]{1,0:T(8,128)(2,1)} %get-tuple-element.10.na_in, f32[72,4608]{1,0:T(8,128)} %get-tuple-element.11.nm_in), custom_call_target="tpu_custom_call" | custom-call | tf_op jit(solution)/shard_map/pallas_call | solution.py:491
